TPU v7x, 32 devices: a whole 2x2x4 slice. The times are simulated.
32 devices in a mesh: groups: 2 (over x), row: 16 (over z, y, core).
Axes of the slice: x: 2, y: 2, z: 4, core: 2. Of those that a mesh axis runs over, the one named last changes fastest.
Arguments:
- root_inverse: float32 [2048, 1024], P(('groups', 'row')), parts along dimension 0, as said below
- root_pivots: float32 [2048], P(('groups', 'row')), parts along dimension 0, may hold values from 0.25 to 4
- pattern: int32 [32, 8, 8], P(('groups', 'row')), parts along dimension 0, may hold values 0 or 1
- cross_factor: float32 [32, 1024, 1024], P('groups', 'row'), parts along dimension 0, may hold values from -0.375 to 0.375
- child_inverse: float32 [32, 512, 2, 1024], P('groups', 'row'), parts along dimension 0, as said below
- child_pivots: float32 [32, 1024], P('groups', 'row'), parts along dimension 0, may hold values from 0.25 to 4
Outputs:
- root_cov: float32 [2048, 1024], P(('groups', 'row')), parts along dimension 0
- cross_cov: float32 [32, 1024, 1024], P('groups', 'row'), parts along dimension 0
- variances: float32 [32, 1024], P(('groups', 'row')), parts along dimension 0
There are 2 independent parts, one for each index of `groups`. A program takes and returns all parts, laid end to end along the dimension named above; each array names one. Nothing has to cross between parts.
Inputs may be any that keep to these rules, and one draw needn't show every extreme that they name: root_inverse is unit lower triangular. `child_inverse`: each G_c, once unfolded, is unit lower triangular.
All inputs are finite; a program needn't handle non-finite values. No bound on the sum of `pattern` on one device may be relied on, other than what follows from the above.
Results may differ from a plain program's by a relative error of at most 0.00009.
Values sent between devices are 32-bit elements; how exact they have to be, the bound alone decides.
No kernel may reach another device: no remote copies, remote signals or barrier semaphores. Data moves between devices by JAX's collectives and lax.ppermute only.
A program may use at most 128 MiB of HBM per device.

v0:
```python
import jax
import jax.numpy as jnp
from jax import lax
from jax.sharding import PartitionSpec as P

BLK = 128


def on_device(root_inverse, root_pivots, pattern, cross_factor, child_inverse, child_pivots):
    hp = lax.Precision.HIGHEST
    count = lax.axis_size("row")
    where = lax.axis_index("row")
    own_rows = root_inverse.shape[0]
    width_root = root_inverse.shape[1]
    piece = lax.all_gather(root_inverse, "row", axis=0, tiled=True)
    pivots = lax.all_gather(root_pivots, "row", axis=0, tiled=True)
    columns = lax.dynamic_slice_in_dim(piece, where * own_rows, own_rows, 1)
    root_cov = jnp.dot(
        columns.T, piece / pivots[:, None], preferred_element_type=jnp.float32, precision=hp
    )
    whole_cov = lax.all_gather(root_cov, "row", axis=0, tiled=True)
    children = cross_factor.shape[0]
    per_device = children // count
    width_child = cross_factor.shape[2]
    fold_rows = child_inverse.shape[1]
    half_rows = width_child // 2
    panel_parts = cross_factor.reshape(count, per_device, own_rows, width_child)
    pivot_parts = child_pivots.reshape(count, per_device, child_pivots.shape[1])
    inverse_parts = child_inverse.reshape(count, per_device, fold_rows, 2 * width_child)
    panels, received, pivots = (
        lax.all_to_all(panel_parts, "row", split_axis=0, concat_axis=2, tiled=True),
        lax.all_to_all(inverse_parts, "row", split_axis=0, concat_axis=2, tiled=True),
        lax.all_to_all(pivot_parts, "row", split_axis=0, concat_axis=2, tiled=True),
    )
    folded = received[0].reshape(per_device, half_rows, 2, width_child)
    inverses = jnp.concatenate([folded[:, :, 0, :], folded[:, ::-1, 1, :]], axis=1)
    panels = panels[0]
    pivots = pivots[0]
    blocks_r = pattern.shape[1]
    blocks_c = pattern.shape[2]
    tall = jnp.broadcast_to(
        pattern[:, :, None, :, None], (per_device, blocks_r, BLK, blocks_c, BLK)
    )
    masks = tall.reshape(per_device, width_root, width_child).astype(jnp.float32)
    masked = panels * masks
    scaled = jnp.einsum(
        "crk,ckj->crj", masked, inverses, preferred_element_type=jnp.float32, precision=hp
    )
    cross = -jnp.einsum(
        "rk,ckj->crj", whole_cov, scaled, preferred_element_type=jnp.float32, precision=hp
    )
    own_part = jnp.sum(inverses * inverses / pivots[:, :, None], axis=1)
    variances = own_part - jnp.sum(scaled * cross, axis=1)
    returned = lax.all_to_all(cross[None], "row", split_axis=2, concat_axis=0, tiled=True)
    cross_cov = returned.reshape(children, own_rows, width_child)
    return (root_cov, cross_cov, variances)


def solution(mesh):
    in_specs = (
        P(("groups", "row"), None),
        P(("groups", "row")),
        P(("groups", "row"), None, None),
        P("groups", "row", None),
        P("groups", "row", None, None),
        P("groups", "row"),
    )
    out_specs = (P(("groups", "row"), None), P("groups", "row", None), P(("groups", "row"), None))
    return jax.shard_map(
        on_device, mesh=mesh, in_specs=in_specs, out_specs=out_specs, check_vma=False
    )
```

profile of v0, /device:TPU:13, one launch (start us, length us, event | category | flops | bytes accessed | tf_op | source)
XLA Modules:
  0.0 450.1 jit_solution(4887532104871562885)
XLA Ops:
  7.2 6.6 %all-to-all-start.3 = ((f32[16,1,64]{2,1,0:T(1,128)}), f32[16,1,64]{2,1,0:T(1,128)S(1)}, u32[]{:S(2)}, u32[]{:S(2)}) async-start(f32[16,1,64]{2,1,0:T(1,128)} %bitcast.43), calls=%async_computation.3 | async-start | bytes 16384 | tf_op jit(solution)/shard_map/all_to_all | solution.py:33
  13.7 6.6 %reshape.155 = f32[16,1,32,2048]{3,2,1,0:T(8,128)} reshape(f32[16,32,2,1024]{3,2,1,0:T(2,128)} %param.10) | data formatting | bytes 8388608 | tf_op jit(solution)/shard_map/reshape | solution.py:29
  20.3 0.0 all-to-all-done.3
  20.3 6.0 %all-to-all-start.1 = ((f32[16,1,32,2048]{3,2,1,0:T(8,128)}), f32[16,1,32,2048]{3,2,1,0:T(8,128)}, u32[]{:S(2)}, u32[]{:S(2)}) async-start(f32[16,1,32,2048]{3,2,1,0:T(8,128)} %reshape.155), calls=%async_computation.1 | async-start | bytes 8388608 | tf_op jit(solution)/shard_map/all_to_all | solution.py:32
  26.4 0.0 all-gather.3.cloned.1.call-start
  26.4 0.7 all-gather.3.cloned.1.call-update
  27.1 117.0 %all-to-all-done.1 = f32[16,1,32,2048]{3,2,1,0:T(8,128)} async-done(((f32[16,1,32,2048]{3,2,1,0:T(8,128)}), f32[16,1,32,2048]{3,2,1,0:T(8,128)}, u32[]{:S(2)}, u32[]{:S(2)}) %all-to-all-start.1) | async-done | bytes 4194336 | tf_op jit(solution)/shard_map/all_to_all | solution.py:32
  144.1 0.0 copy-start.3
  144.1 0.0 copy-start.2
  144.1 5.0 %all-to-all-start = ((f32[16,1,64,1024]{3,2,1,0:T(8,128)}), f32[16,1,64,1024]{3,2,1,0:T(8,128)}, u32[]{:S(2)}, u32[]{:S(2)}) async-start(f32[16,1,64,1024]{3,2,1,0:T(8,128)} %bitcast.38), calls=%async_computation | async-start | bytes 8388608 | tf_op jit(solution)/shard_map/all_to_all | solution.py:31
  149.2 0.0 all-gather.5.cloned.1.call-start
  149.2 0.0 copy-done.3
  149.2 0.6 dynamic-slice
  150.5 0.0 copy-done.2
  150.5 0.2 dynamic-update-slice
  150.7 107.6 %all-reduce = f32[1024]{0:T(1024)S(1)} all-reduce(f32[1024]{0:T(1024)S(1)} %dynamic-update-slice), channel_id=1, replica_groups=mesh['groups'=2,'row'=16] {'row'}, use_global_device_ids=true, to_apply=%add | all-reduce | flops 1024 | bytes 8192
  258.4 0.0 copy-start.1
  258.4 0.0 all-gather.3.cloned.1.call-done
  258.4 6.1 %fusion.4 = f32[64,1024]{1,0:T(8,128)} fusion(f32[1024,1024]{1,0:T(8,128)} %all-gather.3.cloned.1.call-done, f32[1024]{0:T(1024)S(1)} %all-reduce, s32[]{:T(128)S(6)} %select_n.3), kind=kOutput, calls=%fused_computation.7 | convolution fusion | flops 806354944 | bytes 4984836 | tf_op jit(solution)/shard_map/dot_general | solution.py:18
  264.5 0.0 all-gather.5.cloned.1.call-update
  264.5 0.0 copy-done.1
  264.5 0.1 broadcast_in_dim.12
  264.6 0.5 broadcast.32
  265.2 0.7 reduce.5
  265.8 0.1 div.28
  265.9 6.6 %reshape_squeeze.3 = f32[1,512,2,1024]{3,2,1,0:T(2,128)} reshape(f32[16,1,32,2048]{3,2,1,0:T(8,128)} %all-to-all-done.1) | data formatting | bytes 8388608 | tf_op jit(solution)/shard_map/reshape;squeeze | solution.py:35
  272.5 8.6 %slice_bitcast_fusion = (f32[1,512,1024]{2,0,1:T(1,128)}, f32[1,512,1,1024]{3,2,1,0:T(1,128)S(1)}) fusion(f32[1,512,2,1024]{3,2,1,0:T(2,128)} %reshape_squeeze.3), kind=kLoop, calls=%fused_computation.11 | loop fusion | bytes 8388608 | tf_op jit(solution)/shard_map/squeeze | solution.py:36
  281.1 1.4 reverse_bitcast_fusion
  282.5 0.0 all-to-all-done
  282.5 0.0 copy-start
  282.5 3.2 broadcast_multiply_fusion
  285.8 0.0 copy-done
  285.8 12.5 %fusion.6 = (f32[1024]{0:T(1024)S(1)}, f32[1,1024,1024]{2,0,1:T(1,128)S(1)}) fusion(f32[1024]{0:T(1024)S(1)} %div.28, f32[1,512,1024]{2,0,1:T(1,128)S(1)} %reverse_bitcast_fusion, f32[1,512,1024]{2,0,1:T(1,128)S(1)} %copy-done), kind=kLoop, calls=%fused_computation.9 | loop fusion | flops 4193280 | bytes 8396800 | tf_op jit(solution)/shard_map/reduce_sum | solution.py:52
  298.3 15.0 %fusion = f32[1024,1024]{1,0:T(8,128)} fusion(f32[1024,1024]{1,0:T(8,128)S(1)} %bitcast.39, f32[1,1024,1024]{2,0,1:T(1,128)S(1)} %get-tuple-element.4), kind=kOutput, calls=%fused_computation.1 | convolution fusion | flops 12884901888 | bytes 12582912 | tf_op jit(solution)/shard_map/crk,ckj->crj/dot_general | solution.py:46
  313.3 2.0 all-gather.5.cloned.1.call-done
  315.3 17.9 %fusion.3 = (f32[1024]{0:T(1024)S(1)}, f32[1024,1024]{0,1:T(8,128)S(1)}) fusion(f32[1024,1024]{1,0:T(8,128)} %fusion, f32[1024,1024]{1,0:T(8,128)} %all-gather.5.cloned.1.call-done), kind=kOutput, calls=%fused_computation.5 | convolution fusion | flops 12888046592 | bytes 12587008 | tf_op jit(solution)/shard_map/rk,ckj->crj/dot_general | solution.py:49
  333.2 0.4 negate_bitcast_fusion
  333.6 6.3 %copy.11 = f32[1,1,1024,1024]{3,1,0,2:T(1,128)} copy(f32[1,1,1024,1024]{3,2,1,0:T(8,128)S(1)} %negate_bitcast_fusion) | data formatting | bytes 8388608 | tf_op jit(solution)/shard_map/broadcast_in_dim | solution.py:54
  339.9 5.6 %all-to-all-start.2 = ((f32[1,1,1024,1024]{3,1,0,2:T(1,128)}), f32[1,1,1024,1024]{3,1,0,2:T(1,128)}, u32[]{:S(2)}, u32[]{:S(2)}) async-start(f32[1,1,1024,1024]{3,1,0,2:T(1,128)} %copy.11), calls=%async_computation.2 | async-start | bytes 8388608 | tf_op jit(solution)/shard_map/all_to_all | solution.py:54
  345.6 0.6 sub.14
  346.2 91.9 %all-to-all-done.2 = f32[1,1,1024,1024]{3,1,0,2:T(1,128)} async-done(((f32[1,1,1024,1024]{3,1,0,2:T(1,128)}), f32[1,1,1024,1024]{3,1,0,2:T(1,128)}, u32[]{:S(2)}, u32[]{:S(2)}) %all-to-all-start.2) | async-done | bytes 4194336 | tf_op jit(solution)/shard_map/all_to_all | solution.py:54
  438.0 5.2 %copy.13 = f32[1,1,1024,1024]{3,2,0,1:T(8,128)} copy(f32[1,1,1024,1024]{3,1,0,2:T(1,128)} %all-to-all-done.2) | data formatting | bytes 8388608
  (3 shorter events, 0.0 us)
Async XLA Ops:
  7.2 13.2 %all-to-all-start.3 = ((f32[16,1,64]{2,1,0:T(1,128)}), f32[16,1,64]{2,1,0:T(1,128)S(1)}, u32[]{:S(2)}, u32[]{:S(2)}) async-start(f32[16,1,64]{2,1,0:T(1,128)} %bitcast.43), calls=%async_computation.3 | async-start | bytes 16384 | tf_op jit(solution)/shard_map/all_to_all | solution.py:33
  20.3 123.8 %all-to-all-start.1 = ((f32[16,1,32,2048]{3,2,1,0:T(8,128)}), f32[16,1,32,2048]{3,2,1,0:T(8,128)}, u32[]{:S(2)}, u32[]{:S(2)}) async-start(f32[16,1,32,2048]{3,2,1,0:T(8,128)} %reshape.155), calls=%async_computation.1 | async-start | bytes 8388608 | tf_op jit(solution)/shard_map/all_to_all | solution.py:32
  26.4 232.0 %all-gather.3.cloned.1.call-start = ((), (), s32[]{:S(2)}) async-start(), calls=%async_computation.4 | async-start | bytes 4456448 | tf_op jit(solution)/shard_map/all_gather | solution.py:15
  144.1 5.1 %copy-start.3 = (u32[32]{0:T(128)S(1)}, u32[32]{0:T(128)}, u32[]{:S(2)}) copy-start(u32[32]{0:T(128)} %constant.15) | copy-start | bytes 388
  144.1 6.4 %copy-start.2 = (f32[64]{0:T(128)S(1)}, f32[64]{0:T(128)}, u32[]{:S(2)}) copy-start(f32[64]{0:T(128)} %param.7) | copy-start | bytes 772
  144.1 138.4 %all-to-all-start = ((f32[16,1,64,1024]{3,2,1,0:T(8,128)}), f32[16,1,64,1024]{3,2,1,0:T(8,128)}, u32[]{:S(2)}, u32[]{:S(2)}) async-start(f32[16,1,64,1024]{3,2,1,0:T(8,128)} %bitcast.38), calls=%async_computation | async-start | bytes 8388608 | tf_op jit(solution)/shard_map/all_to_all | solution.py:31
  149.2 166.1 %all-gather.5.cloned.1.call-start = ((), (), s32[]{:S(2)}) async-start(), calls=%async_computation.5 | async-start | bytes 4456448 | tf_op jit(solution)/shard_map/all_gather | solution.py:21
  258.4 6.2 %copy-start.1 = (s32[1,8,8]{2,1,0:T(8,128)S(1)}, s32[1,8,8]{2,1,0:T(8,128)}, u32[]{:S(2)}) copy-start(s32[1,8,8]{2,1,0:T(8,128)} %param.8) | copy-start | bytes 772
  282.5 3.2 copy-start
  339.9 98.1 %all-to-all-start.2 = ((f32[1,1,1024,1024]{3,1,0,2:T(1,128)}), f32[1,1,1024,1024]{3,1,0,2:T(1,128)}, u32[]{:S(2)}, u32[]{:S(2)}) async-start(f32[1,1,1024,1024]{3,1,0,2:T(1,128)} %copy.11), calls=%async_computation.2 | async-start | bytes 8388608 | tf_op jit(solution)/shard_map/all_to_all | solution.py:54
Sparse Core Ops, SparseCore 0:
  29.4 94.8 all-gather.2
  264.6 50.5 all-gather.4
where the time goes:
time: 451 us; the launch traced here: 450 us
  waiting for transfers between devices  212 us (47%)
  blocking collectives  108 us (24%)
  matrix products  39 us (9%)
  local copies, waits for them, and re-layouts  36.2 us (8%)
  starting transfers between devices  23.3 us (5%)
  other arithmetic  17.5 us (4%)
  between operations  14.8 us (3%)
    all_to_all x1, waiting for transfers between devices, on_device(): lax.all_to_all(inverse_parts, 'row', split_axis=0, concat_axis=2, tiled=T...  117 us
    unnamed x1, blocking collectives  108 us
    all_to_all x1, waiting for transfers between devices, on_device(): lax.all_to_all(cross[None], 'row', split_axis=2, concat_axis=0, tiled=True)  91.9 us
    dot_general x1, matrix products, on_device(): jnp.einsum('rk,ckj->crj', whole_cov, scaled, preferred_element_type=jnp.f...  17.9 us
    dot_general x1, matrix products, on_device(): jnp.einsum('crk,ckj->crj', masked, inverses, preferred_element_type=jnp.f...  15 us
    reduce_sum x1, other arithmetic, on_device(): own_part = jnp.sum(inverses * inverses / pivots[:, :, None], axis=1)  12.5 us
  transfers between devices with their start and end apart: 6, of which 3 were waited for; matrix products, arithmetic and copies ran while one was open for 14% of the time, Pallas kernels for 0%

commit v1 on v0

v1 whole, which is shorter than its diff:
```python
import jax
import jax.numpy as jnp
from jax import lax
from jax.experimental import pallas as pl
from jax.experimental.pallas import tpu as pltpu
from jax.sharding import PartitionSpec as P

BLK = 128
WIDE = 256
VMEM = 48 * 1024 * 1024


def split(x):
    high = x.astype(jnp.bfloat16)
    return high, (x - high.astype(jnp.float32)).astype(jnp.bfloat16)


def dot(a, b):
    return jnp.dot(a, b, preferred_element_type=jnp.float32)


def dot3(a_high, a_low, b_high, b_low):
    return dot(a_high, b_high) + (dot(a_high, b_low) + dot(a_low, b_high))


def k_range(block, half):
    start = block * WIDE
    if start < half:
        return start, 2 * half
    return half, half + 2 * half - start


def unfold(packed_ref, high_ref, low_ref):
    half, width = packed_ref.shape
    bands = half // BLK
    rows = lax.broadcasted_iota(jnp.int32, (BLK, BLK), 0)
    cols = lax.broadcasted_iota(jnp.int32, (BLK, BLK), 1)
    flip = (rows + cols == BLK - 1).astype(jnp.bfloat16)
    empty = jnp.zeros((BLK, BLK), jnp.bfloat16)
    for q in range(bands):
        here = pl.ds(q * BLK, BLK)
        there = pl.ds(half + q * BLK, BLK)
        last = 2 * bands - 1 - q
        full = packed_ref[here, : last * BLK]
        high_ref[there, : last * BLK], low_ref[there, : last * BLK] = split(full)
        mixed = packed_ref[here, last * BLK : (last + 1) * BLK]
        upper = jnp.where(
            rows + cols < BLK - 1, mixed, (rows + cols == BLK - 1).astype(jnp.float32)
        )
        edge = pl.ds(last * BLK, BLK)
        high_ref[there, edge], low_ref[there, edge] = split(upper)
        if last % 2 == 0:
            after = pl.ds((last + 1) * BLK, BLK)
            high_ref[there, after] = empty
            low_ref[there, after] = empty
        if q:
            rest = packed_ref[here, (last + 1) * BLK :]
            high_ref[here, : q * BLK], low_ref[here, : q * BLK] = split(rest)
        mixed_high, mixed_low = split(mixed)
        edge = pl.ds(q * BLK, BLK)
        diagonal = (rows == cols).astype(jnp.float32)
        high_ref[here, edge] = jnp.where(cols < rows, dot(mixed_high, flip), diagonal).astype(
            jnp.bfloat16
        )
        low_ref[here, edge] = jnp.where(cols < rows, dot(mixed_low, flip), 0.0).astype(
            jnp.bfloat16
        )
        if q % 2 == 0:
            after = pl.ds((q + 1) * BLK, BLK)
            high_ref[here, after] = empty
            low_ref[here, after] = empty


def cross_kernel(t_high_ref, t_low_ref, packed_ref, out_ref, g_high, g_low):
    half, width = packed_ref.shape

    @pl.when(pl.program_id(0) == 0)
    def _():
        unfold(packed_ref, g_high, g_low)

    for block in range(width // WIDE):
        first, stop = k_range(block, half)
        cols = pl.ds(block * WIDE, WIDE)
        out_ref[:, cols] = dot3(
            t_high_ref[:, first:stop],
            t_low_ref[:, first:stop],
            g_high[first:stop, cols],
            g_low[first:stop, cols],
        )


def variance_kernel(m_high_ref, m_low_ref, packed_ref, cross_ref, weight_ref, out_ref, g_high, g_low):
    half, width = packed_ref.shape

    @pl.when(pl.program_id(0) == 0)
    def _():
        unfold(packed_ref, g_high, g_low)
        for block in range(width // WIDE):
            first, stop = k_range(block, half)
            cols = pl.ds(block * WIDE, WIDE)
            entries = g_high[first:stop, cols].astype(jnp.float32) + g_low[
                first:stop, cols
            ].astype(jnp.float32)
            out_ref[:, cols] = jnp.sum(
                entries * entries * weight_ref[first:stop, :], axis=0, keepdims=True
            )

    for block in range(width // WIDE):
        first, stop = k_range(block, half)
        cols = pl.ds(block * WIDE, WIDE)
        scaled = dot3(
            m_high_ref[:, first:stop],
            m_low_ref[:, first:stop],
            g_high[first:stop, cols],
            g_low[first:stop, cols],
        )
        out_ref[:, cols] -= jnp.sum(scaled * cross_ref[:, cols], axis=0, keepdims=True)


def halves(x):
    high = lax.reduce_precision(x, 8, 7)
    return high.astype(jnp.bfloat16), (x - high).astype(jnp.bfloat16)


def pack(child_inverse, where):
    children, fold, _, width = child_inverse.shape
    blocks = width // BLK
    low = child_inverse[:, :, 0, :]
    high = child_inverse[:, :, 1, :]
    q = (where * fold) // BLK
    rows = (where * fold) % BLK + jnp.arange(fold)[:, None]
    spot = jnp.arange(BLK)[None, :]
    low_edge = lax.dynamic_slice_in_dim(low, q * BLK, BLK, 2)[:, :, ::-1]
    moved = lax.dynamic_slice_in_dim(
        jnp.concatenate([low, low], axis=2), q * BLK, width, 2
    )
    high_edge = lax.dynamic_slice_in_dim(high, (blocks - 1 - q) * BLK, BLK, 2)
    edge = jnp.where(spot + rows < BLK - 1, high_edge, low_edge)
    block = jnp.arange(width) // BLK
    packed = jnp.where(block < blocks - 1 - q, high, moved)
    return lax.dynamic_update_slice_in_dim(packed, edge, (blocks - 1 - q) * BLK, 2)


def on_device(root_inverse, root_pivots, pattern, cross_factor, child_inverse, child_pivots):
    count = lax.axis_size("row")
    where = lax.axis_index("row")
    own_rows, width_root = root_inverse.shape
    children, _, width_child = cross_factor.shape
    assert children == count
    half = width_child // 2
    plane = 4
    across = [list(range(k, count, plane)) for k in range(plane)]
    within = [list(range(k, k + plane)) for k in range(0, count, plane)]

    panels = lax.all_to_all(cross_factor, "row", split_axis=0, concat_axis=0, tiled=True)

    factor = root_inverse * lax.rsqrt(root_pivots)[:, None]
    factor = lax.all_gather(factor, "row", axis=0, tiled=True, axis_index_groups=across)
    factor = lax.all_gather(factor, "row", axis=0, tiled=True, axis_index_groups=within)
    pivots = lax.all_gather(child_pivots.reshape(8, -1), "row", axis=0, tiled=True)

    packed = pack(child_inverse, where)
    packed = lax.all_to_all(packed, "row", split_axis=0, concat_axis=0, tiled=True)
    packed = packed.reshape(half, width_child)

    whole_cov = jnp.dot(
        factor.T, factor, preferred_element_type=jnp.float32, precision=lax.Precision.HIGH
    )
    root_cov = lax.dynamic_slice_in_dim(whole_cov, where * own_rows, own_rows, 0)

    mask = jnp.repeat(jnp.repeat(pattern[0], BLK, 0), BLK, 1).astype(jnp.float32)
    masked = panels.reshape(width_root, width_child) * mask
    masked = jnp.concatenate([masked[:, :half], masked[:, half:][:, ::-1]], axis=1)
    turned = -jnp.dot(
        whole_cov, masked, preferred_element_type=jnp.float32, precision=lax.Precision.HIGH
    )
    t_high, t_low = halves(turned)
    m_high, m_low = halves(masked)

    steps = 4
    rows = width_root // steps
    row_spec = pl.BlockSpec((rows, width_child), lambda i: (i, 0))
    whole = lambda *shape: pl.BlockSpec(shape, lambda i: (0, 0))
    scratch = [pltpu.VMEM((width_child, width_child), jnp.bfloat16)] * 2
    flops = 4 * width_root * width_child * width_child
    cross = pl.pallas_call(
        cross_kernel,
        grid=(steps,),
        in_specs=[row_spec, row_spec, whole(half, width_child)],
        out_specs=row_spec,
        out_shape=jax.ShapeDtypeStruct((width_root, width_child), jnp.float32),
        scratch_shapes=scratch,
        compiler_params=pltpu.CompilerParams(vmem_limit_bytes=VMEM),
        cost_estimate=pl.CostEstimate(flops=flops, bytes_accessed=10 << 20, transcendentals=0),
        name="cross",
    )(t_high, t_low, packed)

    returned = lax.all_to_all(
        cross.reshape(children, own_rows, width_child),
        "row",
        split_axis=0,
        concat_axis=0,
        tiled=True,
    )

    mine = lax.dynamic_index_in_dim(pivots.reshape(count, children, own_rows), where, 1, False)
    weights = 1.0 / mine.reshape(width_child)
    weights = jnp.concatenate([weights[:half], weights[half:][::-1]])[:, None]
    variances = pl.pallas_call(
        variance_kernel,
        grid=(steps,),
        in_specs=[
            row_spec,
            row_spec,
            whole(half, width_child),
            row_spec,
            whole(width_child, 1),
        ],
        out_specs=whole(1, width_child),
        out_shape=jax.ShapeDtypeStruct((1, width_child), jnp.float32),
        scratch_shapes=scratch,
        compiler_params=pltpu.CompilerParams(vmem_limit_bytes=VMEM),
        cost_estimate=pl.CostEstimate(flops=flops, bytes_accessed=10 << 20, transcendentals=0),
        name="variance",
    )(m_high, m_low, packed, cross, weights)
    return root_cov, returned, variances


def solution(mesh):
    in_specs = (
        P(("groups", "row"), None),
        P(("groups", "row")),
        P(("groups", "row"), None, None),
        P("groups", "row", None),
        P("groups", "row", None, None),
        P("groups", "row"),
    )
    out_specs = (P(("groups", "row"), None), P("groups", "row", None), P(("groups", "row"), None))
    return jax.shard_map(
        on_device, mesh=mesh, in_specs=in_specs, out_specs=out_specs, check_vma=False
    )
```

time: 451 us -> 319 us (0.71)
  waiting for transfers between devices: 212 us -> 99.7 us
  matrix products: 39 us -> 18.7 us
  Pallas kernels: 0 us -> 16.6 us
  starting transfers between devices: 23.3 us -> 16.4 us
  blocking collectives: 108 us -> 102 us
  other arithmetic: 17.5 us -> 12.9 us
    all_to_all x4 -> x3, waiting for transfers between devices: 209 us -> 41.8 us  [the longest x1 33.4 us: on_device(): lax.all_to_all(cross_factor, 'row', split_axis=0, concat_axis=0, tiled=True)]
    unnamed x1 -> x0, blocking collectives: 108 us -> none
    all_gather x0 -> x1, blocking collectives: none -> 102 us  [on_device(): lax.all_gather(child_pivots.reshape(8, -1), 'row', axis=0, tiled=True)]
    all_gather x2, waiting for transfers between devices: 1.98 us -> 57.8 us  [the longest x1 57.8 us: on_device(): lax.all_gather(factor, 'row', axis=0, tiled=True, axis_index_groups=across)]
    dot_general x3 -> x2, matrix products: 39 us -> 18.7 us  [the longest x1 10.4 us: on_device(): jnp.dot(factor.T, factor, preferred_element_type=jnp.float32, precision=l...]
    pallas_call x0 -> x2, Pallas kernels: none -> 16.6 us  [the longest x1 8.41 us: on_device(): pl.pallas_call(variance_kernel, grid=(steps,), in_specs=[row_spec, row_sp...]
    reduce_sum x1 -> x0, other arithmetic: 12.5 us -> none  [on_device(): own_part = jnp.sum(inverses * inverses / pivots[:, :, None], axis=1)]
    rev x0 -> x3, local copies, waits for them, and re-layouts: none -> 11.9 us  [the longest x1 11.7 us: on_device(): masked[:, half:][:, ::-1]]
  transfers between devices with their start and end apart: 6 -> 5, of which waited for: 3 -> 3; matrix products, arithmetic and copies ran while one was open for 14% -> 19% of each run, Pallas kernels for 0% -> 3%
where the time goes in v1:
time: 319 us; the launch traced here: 317 us
  blocking collectives  102 us (32%)
  waiting for transfers between devices  99.7 us (31%)
  local copies, waits for them, and re-layouts  36.9 us (12%)
  matrix products  18.7 us (6%)
  Pallas kernels  16.6 us (5%)
  starting transfers between devices  16.4 us (5%)
  between operations  14.2 us (4%)
  other arithmetic  12.9 us (4%)
    all_gather x1, blocking collectives, on_device(): lax.all_gather(child_pivots.reshape(8, -1), 'row', axis=0, tiled=True)  102 us
    all_gather x1, waiting for transfers between devices, on_device(): lax.all_gather(factor, 'row', axis=0, tiled=True, axis_index_groups=across)  57.8 us
    all_to_all x1, waiting for transfers between devices, on_device(): lax.all_to_all(cross_factor, 'row', split_axis=0, concat_axis=0, tiled=True)  33.4 us
    unnamed x23, local copies, waits for them, and re-layouts  12.1 us
    rev x1, local copies, waits for them, and re-layouts, on_device(): masked[:, half:][:, ::-1]  11.7 us
    dot_general x1, matrix products, on_device(): jnp.dot(factor.T, factor, preferred_element_type=jnp.float32, precision=l...  10.4 us
    all_to_all x1, waiting for transfers between devices, on_device(): lax.all_to_all(packed, 'row', split_axis=0, concat_axis=0, tiled=True)  8.43 us
    pallas_call x1, Pallas kernels, on_device(): pl.pallas_call(variance_kernel, grid=(steps,), in_specs=[row_spec, row_sp...  8.41 us
  transfers between devices with their start and end apart: 5, of which 3 were waited for; matrix products, arithmetic and copies ran while one was open for 19% of the time, Pallas kernels for 3%

profile of v1, /device:TPU:13, one launch (start us, length us, event | category | flops | bytes accessed | tf_op | source)
XLA Modules:
  0.0 317.3 jit_solution(1100881251515788834)
XLA Ops:
  7.2 0.0 copy-start.9
  7.2 0.0 copy-start.5
  7.2 6.7 %all-to-all-start = ((f32[16,64,1024]{2,1,0:T(8,128)}), f32[16,64,1024]{2,1,0:T(8,128)}, u32[]{:S(2)}, u32[]{:S(2)}) async-start(f32[16,64,1024]{2,1,0:T(8,128)} %param.9), calls=%async_computation | async-start | bytes 8388608 | tf_op jit(solution)/shard_map/all_to_all | solution.py:155
  13.9 0.0 all-gather.3.cloned.1.call-start
  13.9 0.0 copy-done.9
  13.9 0.0 copy-done.5
  14.0 0.8 broadcast_multiply_fusion
  14.7 0.0 all-gather.3.cloned.1.call-update
  14.8 0.0 all-gather.5.cloned.1.call-start
  14.8 57.8 %all-gather.3.cloned.1.call-done = f32[256,1024]{1,0:T(8,128)} async-done(((f32[64,1024]{1,0:T(8,128)}), f32[256,1024]{1,0:T(8,128)}) %all-gather.3.cloned.1.call-update) | async-done | bytes 1048592 | tf_op jit(solution)/shard_map/all_gather | solution.py:158
  72.7 0.0 all-gather.5.cloned.1.call-update
  72.7 7.7 %fusion.11 = (f32[16,32,1,1024]{3,2,1,0:T(1,128)S(1)}, f32[16,32,1,1024]{3,2,1,0:T(1,128)S(1)}) fusion(f32[16,32,2,1024]{3,2,1,0:T(2,128)} %param.10), kind=kLoop, calls=%fused_computation.35 | loop fusion | bytes 8388608 | tf_op jit(solution)/shard_map/slice | solution.py:129
  80.5 0.5 copy.20
  80.9 0.0 copy-start.1
  81.0 1.3 copy-done.1
  82.3 0.1 rev.10
  82.4 1.9 copy.13
  84.3 0.1 add_compare_fusion
  84.4 4.1 %fusion.4 = f32[16,32,1024]{2,1,0:T(8,128)} fusion(s32[]{:T(128)S(6)} %select_n.44, f32[16,32,1024]{2,1,0:T(8,128)} %bitcast.25, pred[1024]{0:T(1024)(128)(4,1)S(1)} %fusion.6, f32[16,32,1,1024]{3,2,1,0:T(1,128)S(1)} %get-tuple-element.7), kind=kLoop, calls=%fused_computation.12 | loop fusion | flops 1048576 | bytes 6292484 | tf_op jit(solution)/shard_map/jit(_where)/select_n | solution.py:140
  88.5 1.7 fusion.5
  90.2 33.4 %all-to-all-done = f32[16,64,1024]{2,1,0:T(8,128)} async-done(((f32[16,64,1024]{2,1,0:T(8,128)}), f32[16,64,1024]{2,1,0:T(8,128)}, u32[]{:S(2)}, u32[]{:S(2)}) %all-to-all-start) | async-done | bytes 4194336 | tf_op jit(solution)/shard_map/all_to_all | solution.py:155
  123.5 4.6 %all-to-all-start.1 = ((f32[16,32,1024]{2,1,0:T(8,128)}), f32[16,32,1024]{2,1,0:T(8,128)}, u32[]{:S(2)}, u32[]{:S(2)}) async-start(f32[16,32,1024]{2,1,0:T(8,128)} %fusion.5), calls=%async_computation.1 | async-start | bytes 4194304 | tf_op jit(solution)/shard_map/all_to_all | solution.py:163
  128.1 0.0 copy-done.8
  128.2 1.1 broadcast_in_dim.21
  129.3 3.7 %bitcast_multiply_fusion = f32[1024,1024]{1,0:T(8,128)S(1)} fusion(f32[128,8,8,128]{3,2,1,0:T(8,128)S(1)} %bitcast.24, f32[16,64,1024]{2,1,0:T(8,128)} %all-to-all-done), kind=kLoop, calls=%fused_computation.6 | loop fusion | flops 1048576 | bytes 12582912 | tf_op jit(solution)/shard_map/mul | solution.py:172
  133.0 1.8 fusion.12
  134.8 11.7 %rev.9 = f32[1024,512]{1,0:T(8,128)} reverse(f32[1024,512]{1,0:T(8,128)S(1)} %get-tuple-element.12), dimensions={1} | reverse | bytes 4194304 | tf_op jit(solution)/shard_map/rev | solution.py:173
  146.5 10.4 %fusion.14 = f32[1024,1024]{1,0:T(8,128)S(1)} fusion(f32[1024,1024]{1,0:T(8,128)} %all-gather.5.cloned.1.call-done), kind=kOutput, calls=%fused_computation.38 | convolution fusion | flops 6442450944 | bytes 8388608 | tf_op jit(solution)/shard_map/dot_general | solution.py:166
  156.9 0.0 copy-start.6
  156.9 2.0 copy-done.6
  158.9 8.3 %fusion = (bf16[1024,1024]{1,0:T(8,128)(2,1)S(1)}, bf16[1024,1024]{1,0:T(8,128)(2,1)}) fusion(f32[1024,1024]{1,0:T(8,128)S(1)} %fusion.14, f32[1024,512]{1,0:T(8,128)S(1)} %copy-done.2, f32[1024,512]{1,0:T(8,128)S(1)} %copy-done.4), kind=kOutput, calls=%fused_computation.4 | convolution fusion | flops 6448742400 | bytes 12582912 | tf_op jit(solution)/shard_map/dot_general | solution.py:174
  167.2 8.4 %all-to-all-done.1 = f32[16,32,1024]{2,1,0:T(8,128)} async-done(((f32[16,32,1024]{2,1,0:T(8,128)}), f32[16,32,1024]{2,1,0:T(8,128)}, u32[]{:S(2)}, u32[]{:S(2)}) %all-to-all-start.1) | async-done | bytes 2097184 | tf_op jit(solution)/shard_map/all_to_all | solution.py:163
  175.6 1.6 copy-done
  177.2 8.2 %cross.1.cross_ref = f32[1024,1024]{1,0:T(8,128)} custom-call(bf16[1024,1024]{1,0:T(8,128)(2,1)S(1)} %copy-done, bf16[1024,1024]{1,0:T(8,128)(2,1)S(1)} %get-tuple-element.9.t_low_ref, f32[512,1024]{1,0:T(8,128)} %bitcast.7.packed_ref), custom_call_target="tpu_custom_call" | custom-call | flops 4294967296 | bytes 10485760 | tf_op jit(solution)/shard_map/cross/pallas_call | solution.py:186
  185.4 5.0 %all-to-all-start.2 = ((f32[16,64,1024]{2,1,0:T(8,128)}), f32[16,64,1024]{2,1,0:T(8,128)}, u32[]{:S(2)}, u32[]{:S(2)}) async-start(f32[16,64,1024]{2,1,0:T(8,128)} %bitcast.26), calls=%async_computation.2 | async-start | bytes 8388608 | tf_op jit(solution)/shard_map/all_to_all | solution.py:198
  190.4 0.1 reshape.43
  190.5 101.9 %all_gather.11 = f32[128,128]{1,0:T(8,128)S(1)} all-gather(f32[8,128]{1,0:T(8,128)S(1)} %reshape.43), channel_id=1, replica_groups=mesh['groups'=2,'row'=16] {'row'}, dimensions={0}, use_global_device_ids=true | all-gather | bytes 69632 | tf_op jit(solution)/shard_map/all_gather | solution.py:160
  292.4 0.1 reshape.44
  292.6 0.1 slice.29
  292.7 0.1 slice.31
  292.7 0.1 rev.11
  292.8 0.2 copy.12.weight_ref
  293.1 1.7 constant_dynamic-slice_fusion
  294.7 0.0 copy-done.3
  294.7 2.5 fusion.1
  297.2 8.4 %variance.1 = f32[1,1024]{1,0:T(1,128)} custom-call(bf16[1024,1024]{1,0:T(8,128)(2,1)S(1)} %get-tuple-element.6.m_high_ref, bf16[1024,1024]{1,0:T(8,128)(2,1)S(1)} %get-tuple-element.5.m_low_ref, f32[512,1024]{1,0:T(8,128)} %bitcast.7.packed_ref, f32[1024,1024]{1,0:T(8,128)} %cross.1.cross_ref, f32[1024,1]{1,0:T(8,128)S(1)} %copy.12.weight_ref), custom_call_target="tpu_custom_call" | custom-call | flops 4294967296 | bytes 10485760 | tf_op jit(solution)/shard_map/variance/pallas_call | solution.py:209
  305.6 0.0 all-to-all-done.2
  305.6 4.8 %copy.23 = f32[16,64,1024]{2,1,0:T(8,128)} copy(f32[16,64,1024]{2,1,0:T(8,128)} %all-to-all-done.2) | data formatting | bytes 8388608
  (19 shorter events, 0.2 us)
Async XLA Ops:
  7.2 6.8 %copy-start.9 = (f32[64]{0:T(128)S(1)}, f32[64]{0:T(128)}, u32[]{:S(2)}) copy-start(f32[64]{0:T(128)} %param.7) | copy-start | bytes 772
  7.2 6.8 %copy-start.5 = (f32[64,1024]{1,0:T(8,128)S(1)}, f32[64,1024]{1,0:T(8,128)}, u32[]{:S(2)}) copy-start(f32[64,1024]{1,0:T(8,128)} %param.6) | copy-start | bytes 786436
  7.2 116.4 %all-to-all-start = ((f32[16,64,1024]{2,1,0:T(8,128)}), f32[16,64,1024]{2,1,0:T(8,128)}, u32[]{:S(2)}, u32[]{:S(2)}) async-start(f32[16,64,1024]{2,1,0:T(8,128)} %param.9), calls=%async_computation | async-start | bytes 8388608 | tf_op jit(solution)/shard_map/all_to_all | solution.py:155
  13.9 58.8 %all-gather.3.cloned.1.call-start = ((), (), s32[]{:S(2)}) async-start(), calls=%async_computation.3 | async-start | bytes 1310720 | tf_op jit(solution)/shard_map/all_gather | solution.py:158
  14.8 131.7 %all-gather.5.cloned.1.call-start = ((), (), s32[]{:S(2)}) async-start(), calls=%async_computation.4 | async-start | bytes 5242880 | tf_op jit(solution)/shard_map/all_gather | solution.py:159
  80.9 1.3 copy-start.1
  84.4 43.7 %copy-start.8 = (s32[1,8,8]{2,1,0:T(8,128)S(1)}, s32[1,8,8]{2,1,0:T(8,128)}, u32[]{:S(2)}) copy-start(s32[1,8,8]{2,1,0:T(8,128)} %param.8) | copy-start | bytes 772
  123.5 52.1 %all-to-all-start.1 = ((f32[16,32,1024]{2,1,0:T(8,128)}), f32[16,32,1024]{2,1,0:T(8,128)}, u32[]{:S(2)}, u32[]{:S(2)}) async-start(f32[16,32,1024]{2,1,0:T(8,128)} %fusion.5), calls=%async_computation.1 | async-start | bytes 4194304 | tf_op jit(solution)/shard_map/all_to_all | solution.py:163
  146.5 12.4 %copy-start.2 = (f32[1024,512]{1,0:T(8,128)S(1)}, f32[1024,512]{1,0:T(8,128)}, u32[]{:S(2)}) copy-start(f32[1024,512]{1,0:T(8,128)} %rev.9) | copy-start | bytes 6291460
  146.5 12.4 %copy-start.4 = (f32[1024,512]{1,0:T(8,128)S(1)}, f32[1024,512]{1,0:T(8,128)}, u32[]{:S(2)}) copy-start(f32[1024,512]{1,0:T(8,128)} %get-tuple-element.11) | copy-start | bytes 6291460
  156.9 2.0 copy-start.6
  175.6 1.6 copy-start
  185.4 5.0 %copy-start.7 = (f32[16,64]{1,0:T(8,128)S(1)}, f32[16,64]{1,0:T(8,128)}, u32[]{:S(2)}) copy-start(f32[16,64]{1,0:T(8,128)} %param.11) | copy-start | bytes 12292
  185.4 109.4 %copy-start.3 = (f32[1024,512]{1,0:T(8,128)S(1)}, f32[1024,512]{1,0:T(8,128)}, u32[]{:S(2)}) copy-start(f32[1024,512]{1,0:T(8,128)} %rev.9) | copy-start | bytes 6291460
  185.4 120.2 %all-to-all-start.2 = ((f32[16,64,1024]{2,1,0:T(8,128)}), f32[16,64,1024]{2,1,0:T(8,128)}, u32[]{:S(2)}, u32[]{:S(2)}) async-start(f32[16,64,1024]{2,1,0:T(8,128)} %bitcast.26), calls=%async_computation.2 | async-start | bytes 8388608 | tf_op jit(solution)/shard_map/all_to_all | solution.py:198
Sparse Core Ops, SparseCore 0:
  16.9 55.7 all-gather.2
  74.2 51.8 all-gather.4

commit v2 on v1

--- a/solution.py
+++ b/solution.py
@@ -7,7 +7,7 @@
 
 BLK = 128
 WIDE = 256
-VMEM = 48 * 1024 * 1024
+VMEM = 60 * 1024 * 1024
 
 
 def split(x):
@@ -155,9 +155,15 @@
     panels = lax.all_to_all(cross_factor, "row", split_axis=0, concat_axis=0, tiled=True)
 
     factor = root_inverse * lax.rsqrt(root_pivots)[:, None]
-    factor = lax.all_gather(factor, "row", axis=0, tiled=True, axis_index_groups=across)
-    factor = lax.all_gather(factor, "row", axis=0, tiled=True, axis_index_groups=within)
-    pivots = lax.all_gather(child_pivots.reshape(8, -1), "row", axis=0, tiled=True)
+    pivot_rows = child_pivots.reshape(-1, width_root)
+    pivot_rows = jnp.pad(pivot_rows, ((0, -pivot_rows.shape[0] % 8), (0, 0)))
+    sent = jnp.concatenate([factor, pivot_rows])
+    sent = lax.all_gather(sent, "row", axis=0, tiled=True, axis_index_groups=across)
+    sent = lax.all_gather(sent, "row", axis=0, tiled=True, axis_index_groups=within)
+    sent = sent.reshape(plane, count // plane, -1, width_root)
+    factor = sent[:, :, :own_rows].reshape(width_root, width_root)
+    pivots = jnp.swapaxes(sent[:, :, own_rows:], 0, 1).reshape(count, -1)
+    pivots = pivots[:, : children * own_rows].reshape(count, children, own_rows)
 
     packed = pack(child_inverse, where)
     packed = lax.all_to_all(packed, "row", split_axis=0, concat_axis=0, tiled=True)
@@ -203,7 +209,7 @@
         tiled=True,
     )
 
-    mine = lax.dynamic_index_in_dim(pivots.reshape(count, children, own_rows), where, 1, False)
+    mine = lax.dynamic_index_in_dim(pivots, where, 1, False)
     weights = 1.0 / mine.reshape(width_child)
     weights = jnp.concatenate([weights[:half], weights[half:][::-1]])[:, None]
     variances = pl.pallas_call(

time: 319 us -> 297 us (0.931)
  blocking collectives: 102 us -> 0 us
  waiting for transfers between devices: 99.7 us -> 171 us
  local copies, waits for them, and re-layouts: 36.9 us -> 41.4 us
    all_gather x1 -> x0, blocking collectives: 102 us -> none  [on_device(): lax.all_gather(child_pivots.reshape(8, -1), 'row', axis=0, tiled=True)]
    all_to_all x1, waiting for transfers between devices: 0.01 us -> 73.9 us  [on_device(): lax.all_to_all(cross.reshape(children, own_rows, width_child), 'row', spl...]
    all_to_all x1, waiting for transfers between devices: 8.43 us -> 4.19 us  [on_device(): lax.all_to_all(packed, 'row', split_axis=0, concat_axis=0, tiled=True)]
    rev x1, local copies, waits for them, and re-layouts: 11.7 us -> 14.9 us  [on_device(): masked[:, half:][:, ::-1]]
    unnamed x23 -> x18, local copies, waits for them, and re-layouts: 12.1 us -> 10.7 us
  transfers between devices with their start and end apart: 5 -> 5, of which waited for: 3 -> 4; matrix products, arithmetic and copies ran while one was open for 19% -> 23% of each run, Pallas kernels for 3% -> 3%
where the time goes in v2:
time: 297 us; the launch traced here: 296 us
  waiting for transfers between devices  171 us (58%)
  local copies, waits for them, and re-layouts  41.4 us (14%)
  matrix products  19 us (6%)
  Pallas kernels  18.4 us (6%)
  starting transfers between devices  16.4 us (6%)
  other arithmetic  15 us (5%)
  between operations  14.3 us (5%)
    all_to_all x1, waiting for transfers between devices, on_device(): lax.all_to_all(cross.reshape(children, own_rows, width_child), 'row', spl...  73.9 us
    all_gather x1, waiting for transfers between devices, on_device(): lax.all_gather(sent, 'row', axis=0, tiled=True, axis_index_groups=across)  60.5 us
    all_to_all x1, waiting for transfers between devices, on_device(): lax.all_to_all(cross_factor, 'row', split_axis=0, concat_axis=0, tiled=True)  32.6 us
    rev x1, local copies, waits for them, and re-layouts, on_device(): masked[:, half:][:, ::-1]  14.9 us
    unnamed x18, local copies, waits for them, and re-layouts  10.7 us
    dot_general x1, matrix products, on_device(): jnp.dot(factor.T, factor, preferred_element_type=jnp.float32, precision=l...  10.4 us
    pallas_call x1, Pallas kernels, on_device(): pl.pallas_call(variance_kernel, grid=(steps,), in_specs=[row_spec, row_sp...  9.45 us
    pallas_call x1, Pallas kernels, on_device(): pl.pallas_call(cross_kernel, grid=(steps,), in_specs=[row_spec, row_spec,...  8.93 us
  transfers between devices with their start and end apart: 5, of which 4 were waited for; matrix products, arithmetic and copies ran while one was open for 23% of the time, Pallas kernels for 3%

profile of v2, /device:TPU:13, one launch (start us, length us, event | category | flops | bytes accessed | tf_op | source)
XLA Modules:
  0.0 295.8 jit_solution(17516966708866123605)
XLA Ops:
  7.2 0.0 copy-start.6
  7.2 0.0 copy-start.4
  7.2 0.0 copy-start.2
  7.2 6.7 %all-to-all-start = ((f32[16,64,1024]{2,1,0:T(8,128)}), f32[16,64,1024]{2,1,0:T(8,128)}, u32[]{:S(2)}, u32[]{:S(2)}) async-start(f32[16,64,1024]{2,1,0:T(8,128)} %param.9), calls=%async_computation | async-start | bytes 8388608 | tf_op jit(solution)/shard_map/all_to_all | solution.py:155
  13.9 0.0 all-gather.3.cloned.1.call-start
  13.9 0.0 copy-done.6
  14.0 0.1 reshape.47
  14.1 0.1 broadcast_multiply_fusion
  14.1 0.7 select_maximum_fusion
  14.9 0.0 all-gather.3.cloned.1.call-update
  14.9 0.0 all-gather.5.cloned.1.call-start
  15.0 60.5 %all-gather.3.cloned.1.call-done = f32[288,1024]{1,0:T(8,128)} async-done(((f32[72,1024]{1,0:T(8,128)}), f32[288,1024]{1,0:T(8,128)}) %all-gather.3.cloned.1.call-update) | async-done | bytes 1179664 | tf_op jit(solution)/shard_map/all_gather | solution.py:161
  75.5 0.0 all-gather.5.cloned.1.call-update
  75.5 7.7 %fusion.16 = (f32[16,32,1,1024]{3,2,1,0:T(1,128)S(1)}, f32[16,32,1,1024]{3,2,1,0:T(1,128)S(1)}) fusion(f32[16,32,2,1024]{3,2,1,0:T(2,128)} %param.10), kind=kLoop, calls=%fused_computation.41 | loop fusion | bytes 8388608 | tf_op jit(solution)/shard_map/slice | solution.py:129
  83.3 0.5 copy.23
  83.8 0.0 copy-start
  83.8 1.3 copy-done
  85.1 0.1 rev.10
  85.2 1.8 copy.15
  87.0 0.1 add_compare_fusion
  87.1 4.1 %fusion.9 = f32[16,32,1024]{2,1,0:T(8,128)} fusion(s32[]{:T(128)S(6)} %select_n.44, f32[16,32,1024]{2,1,0:T(8,128)} %bitcast.33, pred[1024]{0:T(1024)(128)(4,1)S(1)} %fusion.11, f32[16,32,1,1024]{3,2,1,0:T(1,128)S(1)} %get-tuple-element.7), kind=kLoop, calls=%fused_computation.15 | loop fusion | flops 1048576 | bytes 6292484 | tf_op jit(solution)/shard_map/jit(_where)/select_n | solution.py:140
  91.2 1.7 fusion.10
  93.0 32.6 %all-to-all-done = f32[16,64,1024]{2,1,0:T(8,128)} async-done(((f32[16,64,1024]{2,1,0:T(8,128)}), f32[16,64,1024]{2,1,0:T(8,128)}, u32[]{:S(2)}, u32[]{:S(2)}) %all-to-all-start) | async-done | bytes 4194336 | tf_op jit(solution)/shard_map/all_to_all | solution.py:155
  125.6 4.7 %all-to-all-start.1 = ((f32[16,32,1024]{2,1,0:T(8,128)}), f32[16,32,1024]{2,1,0:T(8,128)}, u32[]{:S(2)}, u32[]{:S(2)}) async-start(f32[16,32,1024]{2,1,0:T(8,128)} %fusion.10), calls=%async_computation.1 | async-start | bytes 4194304 | tf_op jit(solution)/shard_map/all_to_all | solution.py:169
  130.4 1.1 broadcast_in_dim.21
  131.5 3.7 %bitcast_multiply_fusion = f32[1024,1024]{1,0:T(8,128)S(1)} fusion(f32[128,8,8,128]{3,2,1,0:T(8,128)S(1)} %bitcast.32, f32[16,64,1024]{2,1,0:T(8,128)} %all-to-all-done), kind=kLoop, calls=%fused_computation.6 | loop fusion | flops 1048576 | bytes 12582912 | tf_op jit(solution)/shard_map/mul | solution.py:178
  135.3 2.4 fusion.17
  137.7 14.9 %rev.9 = f32[1024,512]{1,0:T(8,128)S(1)} reverse(f32[1024,512]{1,0:T(8,128)} %get-tuple-element.12), dimensions={1} | reverse | bytes 4194304 | tf_op jit(solution)/shard_map/rev | solution.py:179
  152.6 0.0 all-gather.5.cloned.1.call-done
  152.7 10.4 %fusion.5 = f32[1024,1024]{1,0:T(8,128)S(1)} fusion(f32[4,4,72,1024]{3,2,1,0:T(8,128)} %bitcast.38), kind=kOutput, calls=%fused_computation.13 | convolution fusion | flops 6442450944 | bytes 8388608 | tf_op jit(solution)/shard_map/dot_general | solution.py:172
  163.1 0.0 copy-start.3
  163.1 2.0 copy-done.3
  165.1 8.6 %fusion = (bf16[1024,1024]{1,0:T(8,128)(2,1)}, bf16[1024,1024]{1,0:T(8,128)(2,1)}) fusion(f32[1024,1024]{1,0:T(8,128)S(1)} %fusion.5, f32[1024,512]{1,0:T(8,128)S(1)} %rev.9, f32[1024,512]{1,0:T(8,128)S(1)} %copy-done.1), kind=kOutput, calls=%fused_computation.4 | convolution fusion | flops 6448742400 | bytes 12582912 | tf_op jit(solution)/shard_map/dot_general | solution.py:180
  173.7 4.2 %all-to-all-done.1 = f32[16,32,1024]{2,1,0:T(8,128)} async-done(((f32[16,32,1024]{2,1,0:T(8,128)}), f32[16,32,1024]{2,1,0:T(8,128)}, u32[]{:S(2)}, u32[]{:S(2)}) %all-to-all-start.1) | async-done | bytes 2097184 | tf_op jit(solution)/shard_map/all_to_all | solution.py:169
  177.9 8.9 %cross.1.cross_ref = f32[1024,1024]{1,0:T(8,128)} custom-call(bf16[1024,1024]{1,0:T(8,128)(2,1)} %get-tuple-element.10.t_high_ref, bf16[1024,1024]{1,0:T(8,128)(2,1)} %get-tuple-element.9.t_low_ref, f32[512,1024]{1,0:T(8,128)} %bitcast.11.packed_ref), custom_call_target="tpu_custom_call" | custom-call | flops 4294967296 | bytes 10485760 | tf_op jit(solution)/shard_map/cross/pallas_call | solution.py:192
  186.8 4.9 %all-to-all-start.2 = ((f32[16,64,1024]{2,1,0:T(8,128)}), f32[16,64,1024]{2,1,0:T(8,128)}, u32[]{:S(2)}, u32[]{:S(2)}) async-start(f32[16,64,1024]{2,1,0:T(8,128)} %bitcast.34), calls=%async_computation.2 | async-start | bytes 8388608 | tf_op jit(solution)/shard_map/all_to_all | solution.py:204
  191.7 4.5 %fusion.1 = (bf16[1024,1024]{1,0:T(8,128)(2,1)}, bf16[1024,1024]{1,0:T(8,128)(2,1)}) fusion(f32[1024,512]{1,0:T(8,128)S(1)} %rev.9, f32[1024,512]{1,0:T(8,128)} %get-tuple-element.11), kind=kLoop, calls=%fused_computation.5 | loop fusion | flops 5242880 | bytes 8388608 | tf_op jit(solution)/shard_map/convert_element_type | solution.py:122
  196.2 1.1 slice_bitcast_fusion
  197.3 0.3 copy.18
  197.7 0.1 reshape.53
  197.8 0.1 slice.41
  197.9 0.1 slice.43
  197.9 0.1 rev.11
  198.1 1.1 copy.13.weight_ref
  199.1 1.7 constant_dynamic-slice_fusion
  200.8 9.4 %variance.1 = f32[1,1024]{1,0:T(1,128)} custom-call(bf16[1024,1024]{1,0:T(8,128)(2,1)} %get-tuple-element.6.m_high_ref, bf16[1024,1024]{1,0:T(8,128)(2,1)} %get-tuple-element.5.m_low_ref, f32[512,1024]{1,0:T(8,128)} %bitcast.11.packed_ref, f32[1024,1024]{1,0:T(8,128)} %cross.1.cross_ref, f32[1024,1]{1,0:T(8,128)} %copy.13.weight_ref), custom_call_target="tpu_custom_call" | custom-call | flops 4294967296 | bytes 10485760 | tf_op jit(solution)/shard_map/variance/pallas_call | solution.py:215
  210.2 73.9 %all-to-all-done.2 = f32[16,64,1024]{2,1,0:T(8,128)} async-done(((f32[16,64,1024]{2,1,0:T(8,128)}), f32[16,64,1024]{2,1,0:T(8,128)}, u32[]{:S(2)}, u32[]{:S(2)}) %all-to-all-start.2) | async-done | bytes 4194336 | tf_op jit(solution)/shard_map/all_to_all | solution.py:204
  284.2 4.8 %copy.26 = f32[16,64,1024]{2,1,0:T(8,128)} copy(f32[16,64,1024]{2,1,0:T(8,128)} %all-to-all-done.2) | data formatting | bytes 8388608
  (17 shorter events, 0.2 us)
Async XLA Ops:
  7.2 6.8 %copy-start.6 = (f32[64]{0:T(128)S(1)}, f32[64]{0:T(128)}, u32[]{:S(2)}) copy-start(f32[64]{0:T(128)} %param.7) | copy-start | bytes 772
  7.2 6.8 %copy-start.4 = (f32[16,64]{1,0:T(8,128)S(1)}, f32[16,64]{1,0:T(8,128)}, u32[]{:S(2)}) copy-start(f32[16,64]{1,0:T(8,128)} %param.11) | copy-start | bytes 12292
  7.2 6.9 %copy-start.2 = (f32[64,1024]{1,0:T(8,128)S(1)}, f32[64,1024]{1,0:T(8,128)}, u32[]{:S(2)}) copy-start(f32[64,1024]{1,0:T(8,128)} %param.6) | copy-start | bytes 786436
  7.2 118.4 %all-to-all-start = ((f32[16,64,1024]{2,1,0:T(8,128)}), f32[16,64,1024]{2,1,0:T(8,128)}, u32[]{:S(2)}, u32[]{:S(2)}) async-start(f32[16,64,1024]{2,1,0:T(8,128)} %param.9), calls=%async_computation | async-start | bytes 8388608 | tf_op jit(solution)/shard_map/all_to_all | solution.py:155
  13.9 61.6 %all-gather.3.cloned.1.call-start = ((), (), s32[]{:S(2)}) async-start(), calls=%async_computation.3 | async-start | bytes 1474560 | tf_op jit(solution)/shard_map/all_gather | solution.py:161
  14.9 137.7 %all-gather.5.cloned.1.call-start = ((), (), s32[]{:S(2)}) async-start(), calls=%async_computation.4 | async-start | bytes 5898240 | tf_op jit(solution)/shard_map/all_gather | solution.py:162
  83.8 1.3 copy-start
  87.1 43.2 %copy-start.5 = (s32[1,8,8]{2,1,0:T(8,128)S(1)}, s32[1,8,8]{2,1,0:T(8,128)}, u32[]{:S(2)}) copy-start(s32[1,8,8]{2,1,0:T(8,128)} %param.8) | copy-start | bytes 772
  125.6 52.2 %all-to-all-start.1 = ((f32[16,32,1024]{2,1,0:T(8,128)}), f32[16,32,1024]{2,1,0:T(8,128)}, u32[]{:S(2)}, u32[]{:S(2)}) async-start(f32[16,32,1024]{2,1,0:T(8,128)} %fusion.10), calls=%async_computation.1 | async-start | bytes 4194304 | tf_op jit(solution)/shard_map/all_to_all | solution.py:169
  152.6 12.5 %copy-start.1 = (f32[1024,512]{1,0:T(8,128)S(1)}, f32[1024,512]{1,0:T(8,128)}, u32[]{:S(2)}) copy-start(f32[1024,512]{1,0:T(8,128)} %get-tuple-element.11) | copy-start | bytes 6291460
  163.1 2.0 copy-start.3
  186.8 97.4 %all-to-all-start.2 = ((f32[16,64,1024]{2,1,0:T(8,128)}), f32[16,64,1024]{2,1,0:T(8,128)}, u32[]{:S(2)}, u32[]{:S(2)}) async-start(f32[16,64,1024]{2,1,0:T(8,128)} %bitcast.34), calls=%async_computation.2 | async-start | bytes 8388608 | tf_op jit(solution)/shard_map/all_to_all | solution.py:204
Sparse Core Ops, SparseCore 0:
  16.9 58.5 all-gather.2
  77.0 53.9 all-gather.4

commit v3 on v2

--- a/solution.py
+++ b/solution.py
@@ -8,6 +8,7 @@
 BLK = 128
 WIDE = 256
 VMEM = 60 * 1024 * 1024
+LIGHT = pl.CostEstimate(flops=1, bytes_accessed=1, transcendentals=0)
 
 
 def split(x):
@@ -71,6 +72,35 @@
             low_ref[here, after] = empty
 
 
+def mask_kernel(pattern_ref, panel_ref, high_ref, low_ref):
+    height, width = panel_ref.shape
+    blocks = width // BLK
+    rows = lax.broadcasted_iota(jnp.int32, (BLK, BLK), 0)
+    cols = lax.broadcasted_iota(jnp.int32, (BLK, BLK), 1)
+    flip = (rows + cols == BLK - 1).astype(jnp.bfloat16)
+    for b in range(blocks):
+        block = panel_ref[:, b * BLK : (b + 1) * BLK]
+        here = pattern_ref[pl.program_id(0), b].astype(jnp.float32)
+        high, low = split(block * here)
+        place = b
+        if b >= blocks // 2:
+            high = dot(high, flip).astype(jnp.bfloat16)
+            low = dot(low, flip).astype(jnp.bfloat16)
+            place = blocks // 2 + blocks - 1 - b
+        to = pl.ds(place * BLK, BLK)
+        high_ref[:, to] = high
+        low_ref[:, to] = low
+
+
+def turn_kernel(cov_ref, m_high_ref, m_low_ref, t_high_ref, t_low_ref):
+    cov_high, cov_low = split(cov_ref[...])
+    for block in range(m_high_ref.shape[1] // WIDE):
+        cols = pl.ds(block * WIDE, WIDE)
+        t_high_ref[:, cols], t_low_ref[:, cols] = split(
+            -dot3(cov_high, cov_low, m_high_ref[:, cols], m_low_ref[:, cols])
+        )
+
+
 def cross_kernel(t_high_ref, t_low_ref, packed_ref, out_ref, g_high, g_low):
     half, width = packed_ref.shape
 
@@ -117,11 +147,6 @@
         out_ref[:, cols] -= jnp.sum(scaled * cross_ref[:, cols], axis=0, keepdims=True)
 
 
-def halves(x):
-    high = lax.reduce_precision(x, 8, 7)
-    return high.astype(jnp.bfloat16), (x - high).astype(jnp.bfloat16)
-
-
 def pack(child_inverse, where):
     children, fold, _, width = child_inverse.shape
     blocks = width // BLK
@@ -141,6 +166,19 @@
     return lax.dynamic_update_slice_in_dim(packed, edge, (blocks - 1 - q) * BLK, 2)
 
 
+def swap(x, count, bit):
+    return lax.ppermute(x, "row", [(i, i ^ bit) for i in range(count)])
+
+
+def spread(held, sources, count, bit):
+    held = jnp.concatenate([held, swap(held, count, bit)])
+    return held, sources + [s ^ bit for s in sources]
+
+
+def exchange(x):
+    return lax.all_to_all(x, "row", split_axis=0, concat_axis=0, tiled=True)
+
+
 def on_device(root_inverse, root_pivots, pattern, cross_factor, child_inverse, child_pivots):
     count = lax.axis_size("row")
     where = lax.axis_index("row")
@@ -148,40 +186,30 @@
     children, _, width_child = cross_factor.shape
     assert children == count
     half = width_child // 2
-    plane = 4
-    across = [list(range(k, count, plane)) for k in range(plane)]
-    within = [list(range(k, k + plane)) for k in range(0, count, plane)]
-
-    panels = lax.all_to_all(cross_factor, "row", split_axis=0, concat_axis=0, tiled=True)
 
     factor = root_inverse * lax.rsqrt(root_pivots)[:, None]
     pivot_rows = child_pivots.reshape(-1, width_root)
     pivot_rows = jnp.pad(pivot_rows, ((0, -pivot_rows.shape[0] % 8), (0, 0)))
-    sent = jnp.concatenate([factor, pivot_rows])
-    sent = lax.all_gather(sent, "row", axis=0, tiled=True, axis_index_groups=across)
-    sent = lax.all_gather(sent, "row", axis=0, tiled=True, axis_index_groups=within)
-    sent = sent.reshape(plane, count // plane, -1, width_root)
-    factor = sent[:, :, :own_rows].reshape(width_root, width_root)
-    pivots = jnp.swapaxes(sent[:, :, own_rows:], 0, 1).reshape(count, -1)
+    packed = pack(child_inverse, where)
+
+    bits = [count // 2, *(1 << k for k in range(1, count.bit_length() - 2)), 1]
+    sent, sources = spread(jnp.concatenate([factor, pivot_rows]), [0], count, bits[0])
+    sent, panels = lax.optimization_barrier((sent, cross_factor))
+    panels = exchange(panels)
+    for bit in bits[1:-1]:
+        sent, sources = spread(sent, sources, count, bit)
+    sent, sources = spread(sent, sources, count, bits[-1])
+    packed = exchange(packed).reshape(half, width_child)
+
+    sent = sent.reshape(count, -1, width_root)
+    factor = sent[:, :own_rows].reshape(width_root, width_root)
+    pivots = sent[:, own_rows:].reshape(count, -1)
     pivots = pivots[:, : children * own_rows].reshape(count, children, own_rows)
-
-    packed = pack(child_inverse, where)
-    packed = lax.all_to_all(packed, "row", split_axis=0, concat_axis=0, tiled=True)
-    packed = packed.reshape(half, width_child)
 
     whole_cov = jnp.dot(
         factor.T, factor, preferred_element_type=jnp.float32, precision=lax.Precision.HIGH
     )
     root_cov = lax.dynamic_slice_in_dim(whole_cov, where * own_rows, own_rows, 0)
-
-    mask = jnp.repeat(jnp.repeat(pattern[0], BLK, 0), BLK, 1).astype(jnp.float32)
-    masked = panels.reshape(width_root, width_child) * mask
-    masked = jnp.concatenate([masked[:, :half], masked[:, half:][:, ::-1]], axis=1)
-    turned = -jnp.dot(
-        whole_cov, masked, preferred_element_type=jnp.float32, precision=lax.Precision.HIGH
-    )
-    t_high, t_low = halves(turned)
-    m_high, m_low = halves(masked)
 
     steps = 4
     rows = width_root // steps
@@ -189,6 +217,32 @@
     whole = lambda *shape: pl.BlockSpec(shape, lambda i: (0, 0))
     scratch = [pltpu.VMEM((width_child, width_child), jnp.bfloat16)] * 2
     flops = 4 * width_root * width_child * width_child
+    halved = jax.ShapeDtypeStruct((width_root, width_child), jnp.bfloat16)
+    band = pl.BlockSpec((BLK, width_child), lambda i: (i, 0))
+    m_high, m_low = pl.pallas_call(
+        mask_kernel,
+        grid=(width_root // BLK,),
+        in_specs=[pl.BlockSpec(memory_space=pltpu.SMEM), band],
+        out_specs=[band, band],
+        out_shape=[halved] * 2,
+        compiler_params=pltpu.CompilerParams(vmem_limit_bytes=VMEM),
+        cost_estimate=LIGHT,
+        name="mask",
+    )(pattern[0], panels.reshape(width_root, width_child))
+    t_high, t_low = pl.pallas_call(
+        turn_kernel,
+        grid=(steps,),
+        in_specs=[
+            pl.BlockSpec((rows, width_root), lambda i: (i, 0)),
+            whole(width_root, width_child),
+            whole(width_root, width_child),
+        ],
+        out_specs=[row_spec, row_spec],
+        out_shape=[halved] * 2,
+        compiler_params=pltpu.CompilerParams(vmem_limit_bytes=VMEM),
+        cost_estimate=LIGHT,
+        name="turn",
+    )(whole_cov, m_high, m_low)
     cross = pl.pallas_call(
         cross_kernel,
         grid=(steps,),
@@ -201,15 +255,12 @@
         name="cross",
     )(t_high, t_low, packed)
 
-    returned = lax.all_to_all(
-        cross.reshape(children, own_rows, width_child),
-        "row",
-        split_axis=0,
-        concat_axis=0,
-        tiled=True,
-    )
+    returned = exchange(cross.reshape(children, own_rows, width_child))
 
     mine = lax.dynamic_index_in_dim(pivots, where, 1, False)
+    owner = jnp.bitwise_xor(where, jnp.array(sources))
+    chosen = (owner[None, :] == jnp.arange(count)[:, None])[:, :, None]
+    mine = jnp.sum(jnp.where(chosen, mine[None], 0.0), axis=1)
     weights = 1.0 / mine.reshape(width_child)
     weights = jnp.concatenate([weights[:half], weights[half:][::-1]])[:, None]
     variances = pl.pallas_call(

time: 297 us -> 284 us (0.956)
  Pallas kernels: 18.4 us -> 36.9 us
  local copies, waits for them, and re-layouts: 41.4 us -> 27.1 us
  between operations: 14.3 us -> 0.78 us
  matrix products: 19 us -> 8.41 us
  starting transfers between devices: 16.4 us -> 26.7 us
  other arithmetic: 15 us -> 11.6 us
    all_gather x2 -> x0, waiting for transfers between devices: 60.5 us -> none  [the longest x1 60.5 us: on_device(): lax.all_gather(sent, 'row', axis=0, tiled=True, axis_index_groups=across)]
    ppermute x0 -> x4, waiting for transfers between devices: none -> 53.3 us  [swap(): return lax.ppermute(x, 'row', [(i, i ^ bit) for i in range(count)])]
    pallas_call x0 -> x2, Pallas kernels: none -> 18.5 us  [the longest x1 11 us: on_device(): pl.pallas_call(turn_kernel, grid=(steps,), in_specs=[pl.BlockSpec((rows,...]
    rev x1 -> x0, local copies, waits for them, and re-layouts: 14.9 us -> none  [on_device(): masked[:, half:][:, ::-1]]
    ppermute x0 -> x4, starting transfers between devices: none -> 9.71 us  [swap(): return lax.ppermute(x, 'row', [(i, i ^ bit) for i in range(count)])]
    dot_general x1 -> x0, matrix products: 8.56 us -> none  [on_device(): jnp.dot(whole_cov, masked, preferred_element_type=jnp.float32, precision=...]
    all_to_all x3, waiting for transfers between devices: 111 us -> 118 us  [exchange(): return lax.all_to_all(x, 'row', split_axis=0, concat_axis=0, tiled=True)]
    convert_element_type x2 -> x0, other arithmetic: 4.51 us -> none  [the longest x1 4.5 us: halves(): return (high.astype(jnp.bfloat16), (x - high).astype(jnp.bfloat16))]
  transfers between devices with their start and end apart: 5 -> 7, of which waited for: 4 -> 6; matrix products, arithmetic and copies ran while one was open for 23% -> 13% of each run, Pallas kernels for 3% -> 10%
where the time goes in v3:
time: 284 us; the launch traced here: 283 us
  waiting for transfers between devices  172 us (61%)
  Pallas kernels  36.9 us (13%)
  local copies, waits for them, and re-layouts  27.1 us (10%)
  starting transfers between devices  26.7 us (9%)
  other arithmetic  11.6 us (4%)
  matrix products  8.41 us (3%)
    all_to_all x3, waiting for transfers between devices, exchange(): return lax.all_to_all(x, 'row', split_axis=0, concat_axis=0, tiled=True)  118 us
    ppermute x4, waiting for transfers between devices, swap(): return lax.ppermute(x, 'row', [(i, i ^ bit) for i in range(count)])  53.3 us
    all_to_all x3, starting transfers between devices, exchange(): return lax.all_to_all(x, 'row', split_axis=0, concat_axis=0, tiled=True)  17 us
    unnamed x14, local copies, waits for them, and re-layouts  11.6 us
    pallas_call x1, Pallas kernels, on_device(): pl.pallas_call(turn_kernel, grid=(steps,), in_specs=[pl.BlockSpec((rows,...  11 us
    ppermute x4, starting transfers between devices, swap(): return lax.ppermute(x, 'row', [(i, i ^ bit) for i in range(count)])  9.71 us
    pallas_call x1, Pallas kernels, on_device(): pl.pallas_call(variance_kernel, grid=(steps,), in_specs=[row_spec, row_sp...  9.45 us
    slice x1, local copies, waits for them, and re-layouts, pack(): high = child_inverse[:, :, 1, :]  9.06 us
  transfers between devices with their start and end apart: 7, of which 6 were waited for; matrix products, arithmetic and copies ran while one was open for 13% of the time, Pallas kernels for 10%

profile of v3, /device:TPU:13, one launch (start us, length us, event | category | flops | bytes accessed | tf_op | source)
XLA Modules:
  0.0 283.3 jit_solution(3353332883786689454)
XLA Ops:
  0.6 0.7 rsqrt.3
  1.3 0.8 reshape.61
  2.1 1.0 broadcast_multiply_fusion
  3.1 2.4 collective-permute-start
  5.5 12.9 %collective-permute-done = f32[72,1024]{1,0:T(8,128)S(1)} collective-permute-done((f32[72,1024]{1,0:T(8,128)S(1)}, f32[72,1024]{1,0:T(8,128)S(1)}, u32[]{:S(2)}, u32[]{:S(2)}) %collective-permute-start) | collective-permute-done | bytes 294944 | tf_op jit(solution)/shard_map/ppermute | solution.py:170
  18.5 7.2 %all-to-all-start = ((f32[16,64,1024]{2,1,0:T(8,128)}), f32[16,64,1024]{2,1,0:T(8,128)}, u32[]{:S(2)}, u32[]{:S(2)}) async-start(f32[16,64,1024]{2,1,0:T(8,128)} %param.10), calls=%async_computation | async-start | bytes 8388608 | tf_op jit(solution)/shard_map/all_to_all | solution.py:179
  25.7 0.3 collective-permute-start.1
  26.0 36.2 %collective-permute-done.1 = f32[144,1024]{1,0:T(8,128)S(1)} collective-permute-done((f32[144,1024]{1,0:T(8,128)S(1)}, f32[144,1024]{1,0:T(8,128)S(1)}, u32[]{:S(2)}, u32[]{:S(2)}) %collective-permute-start.1) | collective-permute-done | bytes 589856 | tf_op jit(solution)/shard_map/ppermute | solution.py:170
  62.2 1.1 pad_maximum_fusion.2
  63.3 6.6 %collective-permute-start.2 = (f32[288,1024]{1,0:T(8,128)}, f32[288,1024]{1,0:T(8,128)}, u32[]{:S(2)}, u32[]{:S(2)}) collective-permute-start(f32[288,1024]{1,0:T(8,128)} %pad_maximum_fusion.2), channel_id=1, source_target_pairs={{0,4},{1,5},{2,6},{3,7},{4,0},{5,1},{6,2},{7,3},{8,12},{9,13},{10,... | collective-permute-start | bytes 3538952 | tf_op jit(solution)/shard_map/ppermute | solution.py:170
  69.9 9.1 %fusion.12 = (f32[16,32,1,1024]{3,2,1,0:T(1,128)S(1)}, f32[16,32,1,1024]{3,2,1,0:T(1,128)}) fusion(f32[16,32,2,1024]{3,2,1,0:T(2,128)} %param.11), kind=kLoop, calls=%fused_computation.34 | loop fusion | bytes 8388608 | tf_op jit(solution)/shard_map/slice | solution.py:154
  79.0 2.1 copy.23
  81.0 0.0 copy-start
  81.0 1.3 copy-done
  82.4 0.8 rev.6
  83.2 1.8 copy.17
  85.0 0.1 add_compare_fusion
  85.1 3.9 %fusion.6 = f32[16,32,1024]{2,1,0:T(8,128)} fusion(s32[]{:T(128)S(6)} %select_n.48, f32[16,32,1024]{2,1,0:T(8,128)} %bitcast.21, pred[1024]{0:T(1024)(128)(4,1)S(1)} %fusion.8, f32[16,32,1,1024]{3,2,1,0:T(1,128)S(1)} %get-tuple-element.15), kind=kLoop, calls=%fused_computation.8 | loop fusion | flops 1048576 | bytes 6292484 | tf_op jit(solution)/shard_map/jit(_where)/select_n | solution.py:165
  89.0 0.0 copy-done.3
  89.0 1.7 fusion.7
  90.7 27.8 %all-to-all-done = f32[16,64,1024]{2,1,0:T(8,128)} async-done(((f32[16,64,1024]{2,1,0:T(8,128)}), f32[16,64,1024]{2,1,0:T(8,128)}, u32[]{:S(2)}, u32[]{:S(2)}) %all-to-all-start) | async-done | bytes 4194336 | tf_op jit(solution)/shard_map/all_to_all | solution.py:179
  118.5 4.8 %all-to-all-start.1 = ((f32[16,32,1024]{2,1,0:T(8,128)}), f32[16,32,1024]{2,1,0:T(8,128)S(1)}, u32[]{:S(2)}, u32[]{:S(2)}) async-start(f32[16,32,1024]{2,1,0:T(8,128)} %fusion.7), calls=%async_computation.1 | async-start | bytes 4194304 | tf_op jit(solution)/shard_map/all_to_all | solution.py:179
  123.3 0.0 collective-permute-done.2
  123.3 1.5 pad_maximum_fusion.1
  124.8 0.4 collective-permute-start.3
  125.2 4.2 %collective-permute-done.3 = f32[576,1024]{1,0:T(8,128)S(1)} collective-permute-done((f32[576,1024]{1,0:T(8,128)S(1)}, f32[576,1024]{1,0:T(8,128)S(1)}, u32[]{:S(2)}, u32[]{:S(2)}) %collective-permute-start.3) | collective-permute-done | bytes 2359328 | tf_op jit(solution)/shard_map/ppermute | solution.py:170
  129.4 2.1 pad_maximum_fusion
  131.5 0.0 copy-start.1
  131.5 8.4 %fusion.2.cov_ref = f32[1024,1024]{1,0:T(8,128)} fusion(f32[16,72,1024]{2,1,0:T(8,128)S(1)} %bitcast.22), kind=kOutput, calls=%fused_computation.6 | convolution fusion | flops 6442450944 | bytes 8388608 | tf_op jit(solution)/shard_map/dot_general | solution.py:209
  139.9 0.0 copy-done.1
  139.9 7.6 %mask.1 = (bf16[1024,1024]{1,0:T(8,128)(2,1)}, bf16[1024,1024]{1,0:T(8,128)(2,1)}) custom-call(s32[8,8]{1,0:T(8,128)} %bitcast.31, f32[1024,1024]{1,0:T(8,128)} %bitcast.3.panel_ref), custom_call_target="tpu_custom_call" | custom-call | flops 1 | bytes 1 | tf_op jit(solution)/shard_map/mask/pallas_call | solution.py:222
  147.5 11.0 %turn.1 = (bf16[1024,1024]{1,0:T(8,128)(2,1)}, bf16[1024,1024]{1,0:T(8,128)(2,1)}) custom-call(f32[1024,1024]{1,0:T(8,128)} %fusion.2.cov_ref, bf16[1024,1024]{1,0:T(8,128)(2,1)} %get-tuple-element.11.m_high_ref, bf16[1024,1024]{1,0:T(8,128)(2,1)} %get-tuple-element.12.m_low_ref), custom_call_target="tpu_custom_call" | custom-call | flops 1 | bytes 1 | tf_op jit(solution)/shard_map/turn/pallas_call | solution.py:232
  158.4 12.3 %all-to-all-done.1 = f32[16,32,1024]{2,1,0:T(8,128)S(1)} async-done(((f32[16,32,1024]{2,1,0:T(8,128)}), f32[16,32,1024]{2,1,0:T(8,128)S(1)}, u32[]{:S(2)}, u32[]{:S(2)}) %all-to-all-start.1) | async-done | bytes 2097184 | tf_op jit(solution)/shard_map/all_to_all | solution.py:179
  170.7 1.3 copy-done.2
  172.0 8.9 %cross.1.cross_ref = f32[1024,1024]{1,0:T(8,128)} custom-call(bf16[1024,1024]{1,0:T(8,128)(2,1)} %get-tuple-element.13.t_high_ref, bf16[1024,1024]{1,0:T(8,128)(2,1)} %get-tuple-element.14.t_low_ref, f32[512,1024]{1,0:T(8,128)} %bitcast.25), custom_call_target="tpu_custom_call" | custom-call | flops 4294967296 | bytes 10485760 | tf_op jit(solution)/shard_map/cross/pallas_call | solution.py:246
  181.0 5.0 %all-to-all-start.2 = ((f32[16,64,1024]{2,1,0:T(8,128)}), f32[16,64,1024]{2,1,0:T(8,128)}, u32[]{:S(2)}, u32[]{:S(2)}) async-start(f32[16,64,1024]{2,1,0:T(8,128)} %bitcast.24), calls=%async_computation.2 | async-start | bytes 8388608 | tf_op jit(solution)/shard_map/all_to_all | solution.py:179
  186.0 1.1 slice.37
  187.1 0.3 copy.19
  187.5 0.1 reshape.67
  187.6 0.1 select_reduce_fusion
  187.7 0.1 slice.33
  187.8 0.1 slice.35
  187.9 0.1 rev.7
  188.0 1.0 copy.16.weight_ref
  189.0 1.7 constant_dynamic-slice_fusion.1
  190.7 9.4 %variance.1 = f32[1,1024]{1,0:T(1,128)} custom-call(bf16[1024,1024]{1,0:T(8,128)(2,1)} %get-tuple-element.11.m_high_ref, bf16[1024,1024]{1,0:T(8,128)(2,1)} %get-tuple-element.12.m_low_ref, f32[512,1024]{1,0:T(8,128)} %bitcast.26, f32[1024,1024]{1,0:T(8,128)} %cross.1.cross_ref, f32[1024,1]{1,0:T(8,128)} %copy.16.weight_ref), custom_call_target="tpu_custom_call" | custom-call | flops 4294967296 | bytes 10485760 | tf_op jit(solution)/shard_map/variance/pallas_call | solution.py:266
  200.1 78.4 %all-to-all-done.2 = f32[16,64,1024]{2,1,0:T(8,128)} async-done(((f32[16,64,1024]{2,1,0:T(8,128)}), f32[16,64,1024]{2,1,0:T(8,128)}, u32[]{:S(2)}, u32[]{:S(2)}) %all-to-all-start.2) | async-done | bytes 4194336 | tf_op jit(solution)/shard_map/all_to_all | solution.py:179
  278.5 4.8 %copy.26 = f32[16,64,1024]{2,1,0:T(8,128)} copy(f32[16,64,1024]{2,1,0:T(8,128)} %all-to-all-done.2) | data formatting | bytes 8388608
  (17 shorter events, 0.2 us)
Async XLA Ops:
  3.1 15.3 %collective-permute-start = (f32[72,1024]{1,0:T(8,128)S(1)}, f32[72,1024]{1,0:T(8,128)S(1)}, u32[]{:S(2)}, u32[]{:S(2)}) collective-permute-start(f32[72,1024]{1,0:T(8,128)S(1)} %pad_maximum_fusion.4), channel_id=1, source_target_pairs={{0,8},{1,9},{2,10},{3,11},{4,12},{5,13},{6,14},{7,15},{8,0},{9,1},... | collective-permute-start | bytes 884744 | tf_op jit(solution)/shard_map/ppermute | solution.py:170
  18.5 100.0 %all-to-all-start = ((f32[16,64,1024]{2,1,0:T(8,128)}), f32[16,64,1024]{2,1,0:T(8,128)}, u32[]{:S(2)}, u32[]{:S(2)}) async-start(f32[16,64,1024]{2,1,0:T(8,128)} %param.10), calls=%async_computation | async-start | bytes 8388608 | tf_op jit(solution)/shard_map/all_to_all | solution.py:179
  25.7 36.5 %collective-permute-start.1 = (f32[144,1024]{1,0:T(8,128)S(1)}, f32[144,1024]{1,0:T(8,128)S(1)}, u32[]{:S(2)}, u32[]{:S(2)}) collective-permute-start(f32[144,1024]{1,0:T(8,128)S(1)} %pad_maximum_fusion.3), channel_id=1, source_target_pairs={{0,2},{1,3},{2,0},{3,1},{4,6},{5,7},{6,4},{7,5},{8,10},{9,11},{10,... | collective-permute-start | bytes 1769480 | tf_op jit(solution)/shard_map/ppermute | solution.py:170
  63.3 60.0 %collective-permute-start.2 = (f32[288,1024]{1,0:T(8,128)}, f32[288,1024]{1,0:T(8,128)}, u32[]{:S(2)}, u32[]{:S(2)}) collective-permute-start(f32[288,1024]{1,0:T(8,128)} %pad_maximum_fusion.2), channel_id=1, source_target_pairs={{0,4},{1,5},{2,6},{3,7},{4,0},{5,1},{6,2},{7,3},{8,12},{9,13},{10,... | collective-permute-start | bytes 3538952 | tf_op jit(solution)/shard_map/ppermute | solution.py:170
  81.0 1.3 copy-start
  85.1 3.9 %copy-start.3 = (f32[16,32,128]{2,1,0:T(8,128)S(1)}, f32[16,32,128]{2,1,0:T(8,128)}, u32[]{:S(2)}) copy-start(f32[16,32,128]{2,1,0:T(8,128)} %rev.6) | copy-start | bytes 786436
  118.5 52.2 %all-to-all-start.1 = ((f32[16,32,1024]{2,1,0:T(8,128)}), f32[16,32,1024]{2,1,0:T(8,128)S(1)}, u32[]{:S(2)}, u32[]{:S(2)}) async-start(f32[16,32,1024]{2,1,0:T(8,128)} %fusion.7), calls=%async_computation.1 | async-start | bytes 4194304 | tf_op jit(solution)/shard_map/all_to_all | solution.py:179
  124.8 4.6 %collective-permute-start.3 = (f32[576,1024]{1,0:T(8,128)S(1)}, f32[576,1024]{1,0:T(8,128)S(1)}, u32[]{:S(2)}, u32[]{:S(2)}) collective-permute-start(f32[576,1024]{1,0:T(8,128)S(1)} %pad_maximum_fusion.1), channel_id=1, source_target_pairs={{0,1},{1,0},{2,3},{3,2},{4,5},{5,4},{6,7},{7,6},{8,9},{9,8},{10,11... | collective-permute-start | bytes 7077896 | tf_op jit(solution)/shard_map/ppermute | solution.py:170
  131.5 8.4 %copy-start.1 = (f32[1152,1024]{1,0:T(8,128)}, f32[1152,1024]{1,0:T(8,128)S(1)}, u32[]{:S(2)}) copy-start(f32[1152,1024]{1,0:T(8,128)S(1)} %pad_maximum_fusion) | copy-start | bytes 14155780
  170.7 1.3 copy-start.2
  181.0 5.0 %copy-start.4 = (s32[16]{0:T(128)S(1)}, s32[16]{0:T(128)}, u32[]{:S(2)}) copy-start(s32[16]{0:T(128)} %constant.66.clone) | copy-start | bytes 196
  181.0 97.5 %all-to-all-start.2 = ((f32[16,64,1024]{2,1,0:T(8,128)}), f32[16,64,1024]{2,1,0:T(8,128)}, u32[]{:S(2)}, u32[]{:S(2)}) async-start(f32[16,64,1024]{2,1,0:T(8,128)} %bitcast.24), calls=%async_computation.2 | async-start | bytes 8388608 | tf_op jit(solution)/shard_map/all_to_all | solution.py:179

commit v4 on v3

--- a/solution.py
+++ b/solution.py
@@ -7,7 +7,9 @@
 
 BLK = 128
 WIDE = 256
-VMEM = 60 * 1024 * 1024
+VMEM = 121 * 512 * 1024
+VMEM_CROSS = 48 * 1024 * 1024
+STEPS = 4
 LIGHT = pl.CostEstimate(flops=1, bytes_accessed=1, transcendentals=0)
 
 
@@ -72,7 +74,7 @@
             low_ref[here, after] = empty
 
 
-def mask_kernel(pattern_ref, panel_ref, high_ref, low_ref):
+def mask_kernel(pattern_ref, panel_ref, m_ref):
     height, width = panel_ref.shape
     blocks = width // BLK
     rows = lax.broadcasted_iota(jnp.int32, (BLK, BLK), 0)
@@ -88,61 +90,93 @@
             low = dot(low, flip).astype(jnp.bfloat16)
             place = blocks // 2 + blocks - 1 - b
         to = pl.ds(place * BLK, BLK)
-        high_ref[:, to] = high
-        low_ref[:, to] = low
-
-
-def turn_kernel(cov_ref, m_high_ref, m_low_ref, t_high_ref, t_low_ref):
+        m_ref[0, :, to] = high
+        m_ref[1, :, to] = low
+
+
+def turn_kernel(cov_ref, m_ref, t_ref):
     cov_high, cov_low = split(cov_ref[...])
-    for block in range(m_high_ref.shape[1] // WIDE):
+    for block in range(m_ref.shape[2] // WIDE):
         cols = pl.ds(block * WIDE, WIDE)
-        t_high_ref[:, cols], t_low_ref[:, cols] = split(
-            -dot3(cov_high, cov_low, m_high_ref[:, cols], m_low_ref[:, cols])
-        )
-
-
-def cross_kernel(t_high_ref, t_low_ref, packed_ref, out_ref, g_high, g_low):
+        t_ref[0, :, cols], t_ref[1, :, cols] = split(
+            -dot3(cov_high, cov_low, m_ref[0, :, cols], m_ref[1, :, cols])
+        )
+
+
+def cross_kernel(t_ref, packed_ref, out_ref, g_ref, t, g, out, came, left, kept):
     half, width = packed_ref.shape
-
-    @pl.when(pl.program_id(0) == 0)
-    def _():
-        unfold(packed_ref, g_high, g_low)
-
-    for block in range(width // WIDE):
-        first, stop = k_range(block, half)
-        cols = pl.ds(block * WIDE, WIDE)
-        out_ref[:, cols] = dot3(
-            t_high_ref[:, first:stop],
-            t_low_ref[:, first:stop],
-            g_high[first:stop, cols],
-            g_low[first:stop, cols],
-        )
-
-
-def variance_kernel(m_high_ref, m_low_ref, packed_ref, cross_ref, weight_ref, out_ref, g_high, g_low):
-    half, width = packed_ref.shape
-
-    @pl.when(pl.program_id(0) == 0)
-    def _():
-        unfold(packed_ref, g_high, g_low)
+    rows = out.shape[0] // STEPS
+    arriving, leaving = [], []
+    for step in range(STEPS):
+        here = pl.ds(step * rows, rows)
+        arriving.append(pltpu.make_async_copy(t_ref.at[:, here], t.at[:, here], came.at[step]))
+        leaving.append(pltpu.make_async_copy(out.at[here], out_ref.at[here], left.at[step]))
+    keeping = pltpu.make_async_copy(g, g_ref, kept)
+    for copy in arriving:
+        copy.start()
+    unfold(packed_ref, g.at[0], g.at[1])
+    keeping.start()
+    for step in range(STEPS):
+        here = pl.ds(step * rows, rows)
+        arriving[step].wait()
         for block in range(width // WIDE):
             first, stop = k_range(block, half)
             cols = pl.ds(block * WIDE, WIDE)
-            entries = g_high[first:stop, cols].astype(jnp.float32) + g_low[
-                first:stop, cols
-            ].astype(jnp.float32)
+            out[here, cols] = dot3(
+                t[0, here, first:stop],
+                t[1, here, first:stop],
+                g[0, first:stop, cols],
+                g[1, first:stop, cols],
+            )
+        leaving[step].start()
+    for copy in leaving:
+        copy.wait()
+    keeping.wait()
+
+
+def copy_kernel(from_ref, to_ref, held, came, left):
+    parts = came.shape[0]
+    each = held.shape[0] // parts
+    pieces = [pl.ds(part * each, each) for part in range(parts)]
+    arriving = [
+        pltpu.make_async_copy(from_ref.at[here], held.at[here], came.at[part])
+        for part, here in enumerate(pieces)
+    ]
+    leaving = [
+        pltpu.make_async_copy(held.at[here], to_ref.at[here], left.at[part])
+        for part, here in enumerate(pieces)
+    ]
+    for copy in arriving:
+        copy.start()
+    for came_in, leave in zip(arriving, leaving):
+        came_in.wait()
+        leave.start()
+    for copy in leaving:
+        copy.wait()
+
+
+def variance_kernel(m_ref, g_ref, cross_ref, weight_ref, out_ref):
+    _, height, width = g_ref.shape
+
+    @pl.when(pl.program_id(0) == 0)
+    def _():
+        for block in range(width // WIDE):
+            first, stop = k_range(block, height // 2)
+            cols = pl.ds(block * WIDE, WIDE)
+            entries = g_ref[0, first:stop, cols].astype(jnp.float32)
+            entries += g_ref[1, first:stop, cols].astype(jnp.float32)
             out_ref[:, cols] = jnp.sum(
                 entries * entries * weight_ref[first:stop, :], axis=0, keepdims=True
             )
 
     for block in range(width // WIDE):
-        first, stop = k_range(block, half)
+        first, stop = k_range(block, height // 2)
         cols = pl.ds(block * WIDE, WIDE)
         scaled = dot3(
-            m_high_ref[:, first:stop],
-            m_low_ref[:, first:stop],
-            g_high[first:stop, cols],
-            g_low[first:stop, cols],
+            m_ref[0, :, first:stop],
+            m_ref[1, :, first:stop],
+            g_ref[0, first:stop, cols],
+            g_ref[1, first:stop, cols],
         )
         out_ref[:, cols] -= jnp.sum(scaled * cross_ref[:, cols], axis=0, keepdims=True)
 
@@ -170,6 +204,13 @@
     return lax.ppermute(x, "row", [(i, i ^ bit) for i in range(count)])
 
 
+def scale(inverse, pivots):
+    rows, width = inverse.shape
+    child_pivots = pivots[0, :-rows].reshape(-1, width)
+    child_pivots = jnp.pad(child_pivots, ((0, -child_pivots.shape[0] % 8), (0, 0)))
+    return inverse * lax.rsqrt(pivots[0, -rows:])[:, None], child_pivots
+
+
 def spread(held, sources, count, bit):
     held = jnp.concatenate([held, swap(held, count, bit)])
     return held, sources + [s ^ bit for s in sources]
@@ -187,18 +228,18 @@
     assert children == count
     half = width_child // 2
 
-    factor = root_inverse * lax.rsqrt(root_pivots)[:, None]
-    pivot_rows = child_pivots.reshape(-1, width_root)
-    pivot_rows = jnp.pad(pivot_rows, ((0, -pivot_rows.shape[0] % 8), (0, 0)))
     packed = pack(child_inverse, where)
 
     bits = [count // 2, *(1 << k for k in range(1, count.bit_length() - 2)), 1]
-    sent, sources = spread(jnp.concatenate([factor, pivot_rows]), [0], count, bits[0])
-    sent, panels = lax.optimization_barrier((sent, cross_factor))
+    pivots = jnp.concatenate([child_pivots.reshape(-1), root_pivots])[None]
+    far_inverse, far_pivots, panels = lax.optimization_barrier(
+        (swap(root_inverse, count, bits[0]), swap(pivots, count, bits[0]), cross_factor)
+    )
+    sent = [*scale(root_inverse, pivots), *scale(far_inverse, far_pivots)]
+    sent, sources = jnp.concatenate(sent), [0, bits[0]]
     panels = exchange(panels)
-    for bit in bits[1:-1]:
+    for bit in bits[1:]:
         sent, sources = spread(sent, sources, count, bit)
-    sent, sources = spread(sent, sources, count, bits[-1])
     packed = exchange(packed).reshape(half, width_child)
 
     sent = sent.reshape(count, -1, width_root)
@@ -211,51 +252,68 @@
     )
     root_cov = lax.dynamic_slice_in_dim(whole_cov, where * own_rows, own_rows, 0)
 
-    steps = 4
-    rows = width_root // steps
+    rows = width_root // STEPS
     row_spec = pl.BlockSpec((rows, width_child), lambda i: (i, 0))
-    whole = lambda *shape: pl.BlockSpec(shape, lambda i: (0, 0))
-    scratch = [pltpu.VMEM((width_child, width_child), jnp.bfloat16)] * 2
-    flops = 4 * width_root * width_child * width_child
-    halved = jax.ShapeDtypeStruct((width_root, width_child), jnp.bfloat16)
+    pair_spec = pl.BlockSpec((2, rows, width_child), lambda i: (0, i, 0))
     band = pl.BlockSpec((BLK, width_child), lambda i: (i, 0))
-    m_high, m_low = pl.pallas_call(
+    pair = jax.ShapeDtypeStruct((2, width_root, width_child), jnp.bfloat16)
+    pair_whole = pl.BlockSpec((2, width_root, width_child), lambda i: (0, 0, 0))
+    anywhere = pl.BlockSpec(memory_space=pltpu.HBM)
+    params = pltpu.CompilerParams(vmem_limit_bytes=VMEM)
+    m = pl.pallas_call(
         mask_kernel,
         grid=(width_root // BLK,),
         in_specs=[pl.BlockSpec(memory_space=pltpu.SMEM), band],
-        out_specs=[band, band],
-        out_shape=[halved] * 2,
-        compiler_params=pltpu.CompilerParams(vmem_limit_bytes=VMEM),
+        out_specs=pl.BlockSpec((2, BLK, width_child), lambda i: (0, i, 0)),
+        out_shape=pair,
+        compiler_params=params,
         cost_estimate=LIGHT,
         name="mask",
     )(pattern[0], panels.reshape(width_root, width_child))
-    t_high, t_low = pl.pallas_call(
+    t = pl.pallas_call(
         turn_kernel,
-        grid=(steps,),
-        in_specs=[
-            pl.BlockSpec((rows, width_root), lambda i: (i, 0)),
-            whole(width_root, width_child),
-            whole(width_root, width_child),
-        ],
-        out_specs=[row_spec, row_spec],
-        out_shape=[halved] * 2,
-        compiler_params=pltpu.CompilerParams(vmem_limit_bytes=VMEM),
+        grid=(STEPS,),
+        in_specs=[pl.BlockSpec((rows, width_root), lambda i: (i, 0)), pair_whole],
+        out_specs=pair_spec,
+        out_shape=pair,
+        compiler_params=params,
         cost_estimate=LIGHT,
         name="turn",
-    )(whole_cov, m_high, m_low)
-    cross = pl.pallas_call(
+    )(whole_cov, m)
+    cross, g = pl.pallas_call(
         cross_kernel,
-        grid=(steps,),
-        in_specs=[row_spec, row_spec, whole(half, width_child)],
-        out_specs=row_spec,
-        out_shape=jax.ShapeDtypeStruct((width_root, width_child), jnp.float32),
-        scratch_shapes=scratch,
-        compiler_params=pltpu.CompilerParams(vmem_limit_bytes=VMEM),
-        cost_estimate=pl.CostEstimate(flops=flops, bytes_accessed=10 << 20, transcendentals=0),
+        in_specs=[anywhere, pl.BlockSpec(memory_space=pltpu.VMEM)],
+        out_specs=[anywhere, anywhere],
+        out_shape=[
+            jax.ShapeDtypeStruct((width_root, width_child), jnp.float32),
+            jax.ShapeDtypeStruct((2, width_child, width_child), jnp.bfloat16),
+        ],
+        scratch_shapes=[
+            pltpu.VMEM((2, width_root, width_child), jnp.bfloat16),
+            pltpu.VMEM((2, width_child, width_child), jnp.bfloat16),
+            pltpu.VMEM((width_root, width_child), jnp.float32),
+            pltpu.SemaphoreType.DMA((STEPS,)),
+            pltpu.SemaphoreType.DMA((STEPS,)),
+            pltpu.SemaphoreType.DMA(()),
+        ],
+        compiler_params=pltpu.CompilerParams(vmem_limit_bytes=VMEM_CROSS),
         name="cross",
-    )(t_high, t_low, packed)
+    )(t, packed)
 
     returned = exchange(cross.reshape(children, own_rows, width_child))
+    returned = pl.pallas_call(
+        copy_kernel,
+        in_specs=[anywhere],
+        out_specs=anywhere,
+        out_shape=jax.ShapeDtypeStruct(returned.shape, returned.dtype),
+        scratch_shapes=[
+            pltpu.VMEM(returned.shape, returned.dtype),
+            pltpu.SemaphoreType.DMA((8,)),
+            pltpu.SemaphoreType.DMA((8,)),
+        ],
+        compiler_params=params,
+        name="place",
+    )(returned)
 
     mine = lax.dynamic_index_in_dim(pivots, where, 1, False)
     owner = jnp.bitwise_xor(where, jnp.array(sources))
@@ -265,21 +323,18 @@
     weights = jnp.concatenate([weights[:half], weights[half:][::-1]])[:, None]
     variances = pl.pallas_call(
         variance_kernel,
-        grid=(steps,),
+        grid=(STEPS,),
         in_specs=[
+            pair_spec,
+            pair_whole,
             row_spec,
-            row_spec,
-            whole(half, width_child),
-            row_spec,
-            whole(width_child, 1),
+            pl.BlockSpec((width_child, 1), lambda i: (0, 0)),
         ],
-        out_specs=whole(1, width_child),
+        out_specs=pl.BlockSpec((1, width_child), lambda i: (0, 0)),
         out_shape=jax.ShapeDtypeStruct((1, width_child), jnp.float32),
-        scratch_shapes=scratch,
-        compiler_params=pltpu.CompilerParams(vmem_limit_bytes=VMEM),
-        cost_estimate=pl.CostEstimate(flops=flops, bytes_accessed=10 << 20, transcendentals=0),
+        compiler_params=params,
         name="variance",
-    )(m_high, m_low, packed, cross, weights)
+    )(m, g, cross, weights)
     return root_cov, returned, variances
 
 

time: 284 us -> 276 us (0.972)
  waiting for transfers between devices: 172 us -> 166 us
  local copies, waits for them, and re-layouts: 27.1 us -> 23.6 us
  other arithmetic: 11.6 us -> 8.2 us
    ppermute x4 -> x5, waiting for transfers between devices: 53.3 us -> 38.3 us  [swap(): return lax.ppermute(x, 'row', [(i, i ^ bit) for i in range(count)])]
    all_to_all x3, waiting for transfers between devices: 118 us -> 128 us  [exchange(): return lax.all_to_all(x, 'row', split_axis=0, concat_axis=0, tiled=True)]
    slice x1, local copies, waits for them, and re-layouts: 9.06 us -> 4.45 us  [pack(): high = child_inverse[:, :, 1, :]]
    concatenate x5 -> x2, other arithmetic: 4.73 us -> 0.7 us  [the longest x1 0.66 us: on_device(): pivots = jnp.concatenate([child_pivots.reshape(-1), root_pivots])[None]]
    concatenate x0 -> x2, local copies, waits for them, and re-layouts: none -> 3.28 us  [spread(): held = jnp.concatenate([held, swap(held, count, bit)])]
    unnamed x14 -> x18, local copies, waits for them, and re-layouts: 11.6 us -> 9.16 us
    pallas_call x3 -> x4, Pallas kernels: 29.3 us -> 30.8 us  [the longest x1 10.8 us: on_device(): pl.pallas_call(turn_kernel, grid=(STEPS,), in_specs=[pl.BlockSpec((rows,...]
    ppermute x4 -> x5, starting transfers between devices: 9.71 us -> 9.77 us  [swap(): return lax.ppermute(x, 'row', [(i, i ^ bit) for i in range(count)])]
  transfers between devices with their start and end apart: 7 -> 8, of which waited for: 6 -> 6; matrix products, arithmetic and copies ran while one was open for 13% -> 15% of each run, Pallas kernels for 10% -> 10%
where the time goes in v4:
time: 276 us; the launch traced here: 275 us
  waiting for transfers between devices  166 us (60%)
  Pallas kernels  38.3 us (14%)
  starting transfers between devices  26.7 us (10%)
  local copies, waits for them, and re-layouts  23.6 us (9%)
  matrix products  11.1 us (4%)
  other arithmetic  8.2 us (3%)
    all_to_all x3, waiting for transfers between devices, exchange(): return lax.all_to_all(x, 'row', split_axis=0, concat_axis=0, tiled=True)  128 us
    ppermute x5, waiting for transfers between devices, swap(): return lax.ppermute(x, 'row', [(i, i ^ bit) for i in range(count)])  38.3 us
    all_to_all x3, starting transfers between devices, exchange(): return lax.all_to_all(x, 'row', split_axis=0, concat_axis=0, tiled=True)  16.9 us
    dot_general x1, matrix products, on_device(): jnp.dot(factor.T, factor, preferred_element_type=jnp.float32, precision=l...  11.1 us
    pallas_call x1, Pallas kernels, on_device(): pl.pallas_call(turn_kernel, grid=(STEPS,), in_specs=[pl.BlockSpec((rows,...  10.8 us
    ppermute x5, starting transfers between devices, swap(): return lax.ppermute(x, 'row', [(i, i ^ bit) for i in range(count)])  9.77 us
    pallas_call x1, Pallas kernels, on_device(): pl.pallas_call(variance_kernel, grid=(STEPS,), in_specs=[pair_spec, pair_...  9.27 us
    unnamed x18, local copies, waits for them, and re-layouts  9.16 us
  transfers between devices with their start and end apart: 8, of which 6 were waited for; matrix products, arithmetic and copies ran while one was open for 15% of the time, Pallas kernels for 10%

profile of v4, /device:TPU:13, one launch (start us, length us, event | category | flops | bytes accessed | tf_op | source)
XLA Modules:
  0.0 275.4 jit_solution(3771691127508486785)
XLA Ops:
  0.6 2.4 collective-permute-start
  3.0 0.8 reshape.72
  3.8 0.7 pad_maximum_fusion.1
  4.4 0.1 collective-permute-start.1
  4.6 10.4 %collective-permute-done.1 = f32[1,1088]{1,0:T(1,128)S(1)} collective-permute-done((f32[1,1088]{1,0:T(1,128)S(1)}, f32[1,1088]{1,0:T(1,128)S(1)}, u32[]{:S(2)}, u32[]{:S(2)}) %collective-permute-start.1) | collective-permute-done | bytes 4384 | tf_op jit(solution)/shard_map/ppermute | solution.py:204
  15.0 7.2 %all-to-all-start = ((f32[16,64,1024]{2,1,0:T(8,128)}), f32[16,64,1024]{2,1,0:T(8,128)}, u32[]{:S(2)}, u32[]{:S(2)}) async-start(f32[16,64,1024]{2,1,0:T(8,128)} %param.10), calls=%async_computation | async-start | bytes 8388608 | tf_op jit(solution)/shard_map/all_to_all | solution.py:220
  22.2 0.8 constant_dynamic-update-slice_fusion.10
  23.0 0.8 constant_dynamic-update-slice_fusion.4
  23.7 0.6 constant_dynamic-update-slice_fusion.3
  24.4 0.8 constant_dynamic-update-slice_fusion.8
  25.2 0.7 constant_dynamic-update-slice_fusion.2
  25.9 0.6 constant_dynamic-update-slice_fusion.7
  26.6 1.0 copy-done.3
  27.6 0.3 collective-permute-start.2
  27.9 4.4 %fusion.13 = (f32[16,32,1,1024]{3,2,1,0:T(1,128)S(1)}, f32[16,32,1,1024]{3,2,1,0:T(1,128)S(1)}) fusion(f32[16,32,2,1024]{3,2,1,0:T(2,128)S(1)} %copy-done), kind=kLoop, calls=%fused_computation.53 | loop fusion | bytes 8388608 | tf_op jit(solution)/shard_map/slice | solution.py:188
  32.3 1.8 copy.23
  34.1 1.0 dynamic-slice_bitcast_fusion
  35.1 23.5 %collective-permute-done.2 = f32[144,1024]{1,0:T(8,128)S(1)} collective-permute-done((f32[144,1024]{1,0:T(8,128)S(1)}, f32[144,1024]{1,0:T(8,128)S(1)}, u32[]{:S(2)}, u32[]{:S(2)}) %collective-permute-start.2) | collective-permute-done | bytes 589856 | tf_op jit(solution)/shard_map/ppermute | solution.py:204
  58.6 1.4 constant_dynamic-update-slice_fusion.6
  60.0 6.6 %collective-permute-start.3 = (f32[288,1024]{1,0:T(8,128)}, f32[288,1024]{1,0:T(8,128)S(1)}, u32[]{:S(2)}, u32[]{:S(2)}) collective-permute-start(f32[288,1024]{1,0:T(8,128)} %get-tuple-element.25), channel_id=1, source_target_pairs={{0,4},{1,5},{2,6},{3,7},{4,0},{5,1},{6,2},{7,3},{8,12},{9,13},{10,... | collective-permute-start | bytes 3538952 | tf_op jit(solution)/shard_map/ppermute | solution.py:204
  66.6 0.8 rev.6
  67.5 1.9 copy.17
  69.5 3.9 %fusion.6 = f32[16,32,1024]{2,1,0:T(8,128)} fusion(s32[]{:T(128)S(6)} %select_n.48, f32[16,32,1024]{2,1,0:T(8,128)} %bitcast.27, pred[1024]{0:T(1024)(128)(4,1)S(1)} %fusion.8, f32[16,32,1,1024]{3,2,1,0:T(1,128)S(1)} %get-tuple-element.17), kind=kLoop, calls=%fused_computation.6 | loop fusion | flops 1048576 | bytes 6292484 | tf_op jit(solution)/shard_map/jit(_where)/select_n | solution.py:199
  73.4 1.7 fusion.7
  75.1 39.8 %all-to-all-done = f32[16,64,1024]{2,1,0:T(8,128)} async-done(((f32[16,64,1024]{2,1,0:T(8,128)}), f32[16,64,1024]{2,1,0:T(8,128)}, u32[]{:S(2)}, u32[]{:S(2)}) %all-to-all-start) | async-done | bytes 4194336 | tf_op jit(solution)/shard_map/all_to_all | solution.py:220
  114.9 4.9 %all-to-all-start.1 = ((f32[16,32,1024]{2,1,0:T(8,128)}), f32[16,32,1024]{2,1,0:T(8,128)S(1)}, u32[]{:S(2)}, u32[]{:S(2)}) async-start(f32[16,32,1024]{2,1,0:T(8,128)} %fusion.7), calls=%async_computation.1 | async-start | bytes 4194304 | tf_op jit(solution)/shard_map/all_to_all | solution.py:220
  119.7 1.7 constant_dynamic-update-slice_fusion.5
  121.4 0.4 collective-permute-start.4
  121.8 4.4 %collective-permute-done.4 = f32[576,1024]{1,0:T(8,128)S(1)} collective-permute-done((f32[576,1024]{1,0:T(8,128)}, f32[576,1024]{1,0:T(8,128)S(1)}, u32[]{:S(2)}, u32[]{:S(2)}) %collective-permute-start.4) | collective-permute-done | bytes 2359328 | tf_op jit(solution)/shard_map/ppermute | solution.py:204
  126.2 1.6 constant_dynamic-update-slice_fusion.11
  127.8 11.1 %fusion.2.cov_ref = f32[1024,1024]{1,0:T(8,128)} fusion(f32[16,72,1024]{2,1,0:T(8,128)} %bitcast.30), kind=kOutput, calls=%fused_computation.4 | convolution fusion | flops 6442450944 | bytes 8388608 | tf_op jit(solution)/shard_map/dot_general | solution.py:250
  138.9 7.5 %mask.1.m_ref = bf16[2,1024,1024]{2,1,0:T(8,128)(2,1)} custom-call(s32[8,8]{1,0:T(8,128)} %bitcast.34, f32[1024,1024]{1,0:T(8,128)} %bitcast.5.panel_ref), custom_call_target="tpu_custom_call" | custom-call | flops 1 | bytes 1 | tf_op jit(solution)/shard_map/mask/pallas_call | solution.py:263
  146.4 10.8 %turn.1.t_ref = bf16[2,1024,1024]{2,1,0:T(8,128)(2,1)} custom-call(f32[1024,1024]{1,0:T(8,128)} %fusion.2.cov_ref, bf16[2,1024,1024]{2,1,0:T(8,128)(2,1)} %mask.1.m_ref), custom_call_target="tpu_custom_call" | custom-call | flops 1 | bytes 1 | tf_op jit(solution)/shard_map/turn/pallas_call | solution.py:273
  157.2 9.9 %all-to-all-done.1 = f32[16,32,1024]{2,1,0:T(8,128)S(1)} async-done(((f32[16,32,1024]{2,1,0:T(8,128)}), f32[16,32,1024]{2,1,0:T(8,128)S(1)}, u32[]{:S(2)}, u32[]{:S(2)}) %all-to-all-start.1) | async-done | bytes 2097184 | tf_op jit(solution)/shard_map/all_to_all | solution.py:220
  167.1 7.1 %cross.1 = (f32[1024,1024]{1,0:T(8,128)}, bf16[2,1024,1024]{2,1,0:T(8,128)(2,1)}) custom-call(bf16[2,1024,1024]{2,1,0:T(8,128)(2,1)} %turn.1.t_ref, f32[512,1024]{1,0:T(8,128)S(1)} %bitcast.25), custom_call_target="tpu_custom_call" | custom-call | tf_op jit(solution)/shard_map/cross/pallas_call | solution.py:283
  174.3 4.9 %all-to-all-start.2 = ((f32[16,64,1024]{2,1,0:T(8,128)}), f32[16,64,1024]{2,1,0:T(8,128)}, u32[]{:S(2)}, u32[]{:S(2)}) async-start(f32[16,64,1024]{2,1,0:T(8,128)} %bitcast.26), calls=%async_computation.2 | async-start | bytes 8388608 | tf_op jit(solution)/shard_map/all_to_all | solution.py:220
  179.2 1.1 slice.55
  180.3 0.3 copy.19
  180.6 0.1 reshape.78
  180.7 0.1 select_reduce_fusion
  180.9 0.1 slice.49
  180.9 0.1 slice.51
  181.0 0.1 rev.7
  181.1 1.0 copy.16.weight_ref
  182.2 1.7 constant_dynamic-slice_fusion.1
  183.8 9.3 %variance.1 = f32[1,1024]{1,0:T(1,128)} custom-call(bf16[2,1024,1024]{2,1,0:T(8,128)(2,1)} %mask.1.m_ref, bf16[2,1024,1024]{2,1,0:T(8,128)(2,1)} %get-tuple-element.12.g_ref, f32[1024,1024]{1,0:T(8,128)} %get-tuple-element.11.cross_ref, f32[1024,1]{1,0:T(8,128)} %copy.16.weight_ref), custom_call_target="tpu_custom_call" | custom-call | tf_op jit(solution)/shard_map/variance/pallas_call | solution.py:324
  193.1 78.5 %all-to-all-done.2.from_ref = f32[16,64,1024]{2,1,0:T(8,128)} async-done(((f32[16,64,1024]{2,1,0:T(8,128)}), f32[16,64,1024]{2,1,0:T(8,128)}, u32[]{:S(2)}, u32[]{:S(2)}) %all-to-all-start.2) | async-done | bytes 4194336 | tf_op jit(solution)/shard_map/all_to_all | solution.py:220
  271.6 3.6 %place.1 = f32[16,64,1024]{2,1,0:T(8,128)} custom-call(f32[16,64,1024]{2,1,0:T(8,128)} %all-to-all-done.2.from_ref), custom_call_target="tpu_custom_call" | custom-call | tf_op jit(solution)/shard_map/place/pallas_call | solution.py:304
  (27 shorter events, 0.2 us)
Async XLA Ops:
  0.6 14.3 %collective-permute-start = (f32[64,1024]{1,0:T(8,128)}, f32[64,1024]{1,0:T(8,128)S(1)}, u32[]{:S(2)}, u32[]{:S(2)}) collective-permute-start(f32[64,1024]{1,0:T(8,128)} %param.7), channel_id=1, source_target_pairs={{0,8},{1,9},{2,10},{3,11},{4,12},{5,13},{6,14},{7,15},{8,0},{9,1},... | collective-permute-start | bytes 786440 | tf_op jit(solution)/shard_map/ppermute | solution.py:204
  4.4 17.7 %copy-start.2 = (f32[64,1024]{1,0:T(8,128)S(1)}, f32[64,1024]{1,0:T(8,128)}, u32[]{:S(2)}) copy-start(f32[64,1024]{1,0:T(8,128)} %param.7) | copy-start | bytes 786436
  4.4 10.5 %collective-permute-start.1 = (f32[1,1088]{1,0:T(1,128)S(1)}, f32[1,1088]{1,0:T(1,128)S(1)}, u32[]{:S(2)}, u32[]{:S(2)}) collective-permute-start(f32[1,1088]{1,0:T(1,128)S(1)} %broadcast_in_dim.44), channel_id=1, source_target_pairs={{0,8},{1,9},{2,10},{3,11},{4,12},{5,13},{6,14},{7,15},{8,0},{9,1},... | collective-permute-start | bytes 13064 | tf_op jit(solution)/shard_map/ppermute | solution.py:204
  15.0 99.9 %all-to-all-start = ((f32[16,64,1024]{2,1,0:T(8,128)}), f32[16,64,1024]{2,1,0:T(8,128)}, u32[]{:S(2)}, u32[]{:S(2)}) async-start(f32[16,64,1024]{2,1,0:T(8,128)} %param.10), calls=%async_computation | async-start | bytes 8388608 | tf_op jit(solution)/shard_map/all_to_all | solution.py:220
  22.1 5.7 %copy-start = (f32[16,32,2,1024]{3,2,1,0:T(2,128)S(1)}, f32[16,32,2,1024]{3,2,1,0:T(2,128)}, u32[]{:S(2)}) copy-start(f32[16,32,2,1024]{3,2,1,0:T(2,128)} %param.11) | copy-start | bytes 12582916
  26.6 1.0 copy-start.3
  27.6 31.0 %collective-permute-start.2 = (f32[144,1024]{1,0:T(8,128)S(1)}, f32[144,1024]{1,0:T(8,128)S(1)}, u32[]{:S(2)}, u32[]{:S(2)}) collective-permute-start(f32[144,1024]{1,0:T(8,128)S(1)} %pad_maximum_fusion), channel_id=1, source_target_pairs={{0,2},{1,3},{2,0},{3,1},{4,6},{5,7},{6,4},{7,5},{8,10},{9,11},{10,... | collective-permute-start | bytes 1769480 | tf_op jit(solution)/shard_map/ppermute | solution.py:204
  60.0 59.7 %collective-permute-start.3 = (f32[288,1024]{1,0:T(8,128)}, f32[288,1024]{1,0:T(8,128)S(1)}, u32[]{:S(2)}, u32[]{:S(2)}) collective-permute-start(f32[288,1024]{1,0:T(8,128)} %get-tuple-element.25), channel_id=1, source_target_pairs={{0,4},{1,5},{2,6},{3,7},{4,0},{5,1},{6,2},{7,3},{8,12},{9,13},{10,... | collective-permute-start | bytes 3538952 | tf_op jit(solution)/shard_map/ppermute | solution.py:204
  69.4 3.9 %copy-start.1 = (f32[16,32,128]{2,1,0:T(8,128)S(1)}, f32[16,32,128]{2,1,0:T(8,128)}, u32[]{:S(2)}) copy-start(f32[16,32,128]{2,1,0:T(8,128)} %rev.6) | copy-start | bytes 786436
  114.9 52.3 %all-to-all-start.1 = ((f32[16,32,1024]{2,1,0:T(8,128)}), f32[16,32,1024]{2,1,0:T(8,128)S(1)}, u32[]{:S(2)}, u32[]{:S(2)}) async-start(f32[16,32,1024]{2,1,0:T(8,128)} %fusion.7), calls=%async_computation.1 | async-start | bytes 4194304 | tf_op jit(solution)/shard_map/all_to_all | solution.py:220
  121.4 4.7 %collective-permute-start.4 = (f32[576,1024]{1,0:T(8,128)}, f32[576,1024]{1,0:T(8,128)S(1)}, u32[]{:S(2)}, u32[]{:S(2)}) collective-permute-start(f32[576,1024]{1,0:T(8,128)} %get-tuple-element.21), channel_id=1, source_target_pairs={{0,1},{1,0},{2,3},{3,2},{4,5},{5,4},{6,7},{7,6},{8,9},{9,8},{10,11... | collective-permute-start | bytes 7077896 | tf_op jit(solution)/shard_map/ppermute | solution.py:204
  174.2 4.9 %copy-start.4 = (s32[16]{0:T(128)S(1)}, s32[16]{0:T(128)}, u32[]{:S(2)}) copy-start(s32[16]{0:T(128)} %constant.66.clone) | copy-start | bytes 196
  174.3 97.4 %all-to-all-start.2 = ((f32[16,64,1024]{2,1,0:T(8,128)}), f32[16,64,1024]{2,1,0:T(8,128)}, u32[]{:S(2)}, u32[]{:S(2)}) async-start(f32[16,64,1024]{2,1,0:T(8,128)} %bitcast.26), calls=%async_computation.2 | async-start | bytes 8388608 | tf_op jit(solution)/shard_map/all_to_all | solution.py:220

commit v5 on v4

--- a/solution.py
+++ b/solution.py
@@ -72,6 +72,26 @@
             after = pl.ds((q + 1) * BLK, BLK)
             high_ref[here, after] = empty
             low_ref[here, after] = empty
+
+
+def cov_kernel(sent_ref, cov_ref, high_ref, low_ref):
+    count = sent_ref.shape[0]
+    width = high_ref.shape[1]
+    own = high_ref.shape[0] // count
+    rows = cov_ref.shape[0]
+
+    @pl.when(pl.program_id(0) == 0)
+    def _():
+        for s in range(count):
+            here = pl.ds(s * own, own)
+            high_ref[here, :], low_ref[here, :] = split(sent_ref[s, :own, :])
+
+    mine = pl.ds(pl.multiple_of(pl.program_id(0) * rows, rows), rows)
+    left_high = high_ref[:, mine].T
+    left_low = low_ref[:, mine].T
+    for block in range(width // WIDE):
+        cols = pl.ds(block * WIDE, WIDE)
+        cov_ref[:, cols] = dot3(left_high, left_low, high_ref[:, cols], low_ref[:, cols])
 
 
 def mask_kernel(pattern_ref, panel_ref, m_ref):
@@ -243,14 +263,8 @@
     packed = exchange(packed).reshape(half, width_child)
 
     sent = sent.reshape(count, -1, width_root)
-    factor = sent[:, :own_rows].reshape(width_root, width_root)
     pivots = sent[:, own_rows:].reshape(count, -1)
     pivots = pivots[:, : children * own_rows].reshape(count, children, own_rows)
-
-    whole_cov = jnp.dot(
-        factor.T, factor, preferred_element_type=jnp.float32, precision=lax.Precision.HIGH
-    )
-    root_cov = lax.dynamic_slice_in_dim(whole_cov, where * own_rows, own_rows, 0)
 
     rows = width_root // STEPS
     row_spec = pl.BlockSpec((rows, width_child), lambda i: (i, 0))
@@ -260,6 +274,19 @@
     pair_whole = pl.BlockSpec((2, width_root, width_child), lambda i: (0, 0, 0))
     anywhere = pl.BlockSpec(memory_space=pltpu.HBM)
     params = pltpu.CompilerParams(vmem_limit_bytes=VMEM)
+    whole_cov = pl.pallas_call(
+        cov_kernel,
+        grid=(STEPS,),
+        in_specs=[pl.BlockSpec(sent.shape, lambda i: (0, 0, 0))],
+        out_specs=pl.BlockSpec((rows, width_root), lambda i: (i, 0)),
+        out_shape=jax.ShapeDtypeStruct((width_root, width_root), jnp.float32),
+        scratch_shapes=[pltpu.VMEM((width_root, width_root), jnp.bfloat16)] * 2,
+        compiler_params=params,
+        cost_estimate=pl.CostEstimate(flops=6 * width_root**3, bytes_accessed=16 << 20, transcendentals=0),
+        name="cov",
+    )(sent)
+    root_cov = lax.dynamic_slice_in_dim(whole_cov, where * own_rows, own_rows, 0)
+
     m = pl.pallas_call(
         mask_kernel,
         grid=(width_root // BLK,),

time: 276 us -> 276 us (level)
  Pallas kernels: 38.3 us -> 49.6 us
  matrix products: 11.1 us -> 0 us
    pallas_call x0 -> x1, Pallas kernels: none -> 11.3 us  [on_device(): pl.pallas_call(cov_kernel, grid=(STEPS,), in_specs=[pl.BlockSpec(sent.sha...]
    dot_general x1 -> x0, matrix products: 11.1 us -> none  [on_device(): jnp.dot(factor.T, factor, preferred_element_type=jnp.float32, precision=l...]
    ppermute x5, waiting for transfers between devices: 38.3 us -> 35.1 us  [swap(): return lax.ppermute(x, 'row', [(i, i ^ bit) for i in range(count)])]
    all_to_all x3, waiting for transfers between devices: 128 us -> 131 us  [exchange(): return lax.all_to_all(x, 'row', split_axis=0, concat_axis=0, tiled=True)]
    unnamed x18 -> x20, local copies, waits for them, and re-layouts: 9.16 us -> 10.8 us
  transfers between devices with their start and end apart: 8 -> 8, of which waited for: 6 -> 6; matrix products, arithmetic and copies ran while one was open for 15% -> 11% of each run, Pallas kernels for 10% -> 14%
where the time goes in v5:
time: 276 us; the launch traced here: 275 us
  waiting for transfers between devices  166 us (60%)
  Pallas kernels  49.6 us (18%)
  starting transfers between devices  26.8 us (10%)
  local copies, waits for them, and re-layouts  25 us (9%)
  other arithmetic  6.61 us (2%)
    all_to_all x3, waiting for transfers between devices, exchange(): return lax.all_to_all(x, 'row', split_axis=0, concat_axis=0, tiled=True)  131 us
    ppermute x5, waiting for transfers between devices, swap(): return lax.ppermute(x, 'row', [(i, i ^ bit) for i in range(count)])  35.1 us
    all_to_all x3, starting transfers between devices, exchange(): return lax.all_to_all(x, 'row', split_axis=0, concat_axis=0, tiled=True)  16.9 us
    pallas_call x1, Pallas kernels, on_device(): pl.pallas_call(cov_kernel, grid=(STEPS,), in_specs=[pl.BlockSpec(sent.sha...  11.3 us
    unnamed x20, local copies, waits for them, and re-layouts  10.8 us
    pallas_call x1, Pallas kernels, on_device(): pl.pallas_call(turn_kernel, grid=(STEPS,), in_specs=[pl.BlockSpec((rows,...  10.8 us
    ppermute x5, starting transfers between devices, swap(): return lax.ppermute(x, 'row', [(i, i ^ bit) for i in range(count)])  9.83 us
    pallas_call x1, Pallas kernels, on_device(): pl.pallas_call(variance_kernel, grid=(STEPS,), in_specs=[pair_spec, pair_...  9.27 us
  transfers between devices with their start and end apart: 8, of which 6 were waited for; matrix products, arithmetic and copies ran while one was open for 11% of the time, Pallas kernels for 14%

profile of v5, /device:TPU:13, one launch (start us, length us, event | category | flops | bytes accessed | tf_op | source)
XLA Modules:
  0.0 275.4 jit_solution(9440816788873643290)
XLA Ops:
  0.6 2.4 collective-permute-start
  3.0 0.8 reshape.71
  3.8 0.7 pad_maximum_fusion.1
  4.4 0.1 collective-permute-start.1
  4.6 10.4 %collective-permute-done.1 = f32[1,1088]{1,0:T(1,128)S(1)} collective-permute-done((f32[1,1088]{1,0:T(1,128)S(1)}, f32[1,1088]{1,0:T(1,128)S(1)}, u32[]{:S(2)}, u32[]{:S(2)}) %collective-permute-start.1) | collective-permute-done | bytes 4384 | tf_op jit(solution)/shard_map/ppermute | solution.py:224
  15.0 7.2 %all-to-all-start = ((f32[16,64,1024]{2,1,0:T(8,128)}), f32[16,64,1024]{2,1,0:T(8,128)}, u32[]{:S(2)}, u32[]{:S(2)}) async-start(f32[16,64,1024]{2,1,0:T(8,128)} %param.10), calls=%async_computation | async-start | bytes 8388608 | tf_op jit(solution)/shard_map/all_to_all | solution.py:240
  22.2 0.8 constant_dynamic-update-slice_fusion.10
  23.0 0.8 constant_dynamic-update-slice_fusion.4
  23.7 0.6 constant_dynamic-update-slice_fusion.3
  24.3 0.8 constant_dynamic-update-slice_fusion.8
  25.2 0.8 constant_dynamic-update-slice_fusion.2
  25.9 0.6 constant_dynamic-update-slice_fusion.7
  26.6 0.3 collective-permute-start.2
  27.0 5.8 %fusion.8 = (f32[16,32,1,1024]{3,2,1,0:T(1,128)S(1)}, f32[16,32,1,1024]{3,2,1,0:T(1,128)}) fusion(f32[16,32,2,1024]{3,2,1,0:T(2,128)S(1)} %copy-done.2), kind=kLoop, calls=%fused_computation.50 | loop fusion | bytes 8388608 | tf_op jit(solution)/shard_map/slice | solution.py:208
  32.7 2.1 copy.23
  34.8 1.4 copy-done
  36.3 0.1 rev.6
  36.4 1.8 copy.17
  38.2 0.1 add_compare_fusion
  38.3 20.3 %collective-permute-done.2 = f32[144,1024]{1,0:T(8,128)} collective-permute-done((f32[144,1024]{1,0:T(8,128)S(1)}, f32[144,1024]{1,0:T(8,128)}, u32[]{:S(2)}, u32[]{:S(2)}) %collective-permute-start.2) | collective-permute-done | bytes 589856 | tf_op jit(solution)/shard_map/ppermute | solution.py:224
  58.6 2.5 constant_dynamic-update-slice_fusion.6
  61.1 6.6 %collective-permute-start.3 = (f32[288,1024]{1,0:T(8,128)}, f32[288,1024]{1,0:T(8,128)S(1)}, u32[]{:S(2)}, u32[]{:S(2)}) collective-permute-start(f32[288,1024]{1,0:T(8,128)} %get-tuple-element.25), channel_id=1, source_target_pairs={{0,4},{1,5},{2,6},{3,7},{4,0},{5,1},{6,2},{7,3},{8,12},{9,13},{10,... | collective-permute-start | bytes 3538952 | tf_op jit(solution)/shard_map/ppermute | solution.py:224
  67.7 2.4 fusion.1
  70.1 1.7 fusion.2
  71.8 43.1 %all-to-all-done = f32[16,64,1024]{2,1,0:T(8,128)} async-done(((f32[16,64,1024]{2,1,0:T(8,128)}), f32[16,64,1024]{2,1,0:T(8,128)}, u32[]{:S(2)}, u32[]{:S(2)}) %all-to-all-start) | async-done | bytes 4194336 | tf_op jit(solution)/shard_map/all_to_all | solution.py:240
  114.9 4.9 %all-to-all-start.1 = ((f32[16,32,1024]{2,1,0:T(8,128)}), f32[16,32,1024]{2,1,0:T(8,128)S(1)}, u32[]{:S(2)}, u32[]{:S(2)}) async-start(f32[16,32,1024]{2,1,0:T(8,128)} %fusion.2), calls=%async_computation.1 | async-start | bytes 4194304 | tf_op jit(solution)/shard_map/all_to_all | solution.py:240
  119.7 1.7 constant_dynamic-update-slice_fusion.5
  121.4 0.4 collective-permute-start.4
  121.8 4.4 %collective-permute-done.4 = f32[576,1024]{1,0:T(8,128)S(1)} collective-permute-done((f32[576,1024]{1,0:T(8,128)}, f32[576,1024]{1,0:T(8,128)S(1)}, u32[]{:S(2)}, u32[]{:S(2)}) %collective-permute-start.4) | collective-permute-done | bytes 2359328 | tf_op jit(solution)/shard_map/ppermute | solution.py:224
  126.2 1.6 constant_dynamic-update-slice_fusion.11
  127.8 11.3 %cov.1.cov_ref = f32[1024,1024]{1,0:T(8,128)} custom-call(f32[16,72,1024]{2,1,0:T(8,128)} %bitcast.28), custom_call_target="tpu_custom_call" | custom-call | flops 6442450944 | bytes 16777216 | tf_op jit(solution)/shard_map/cov/pallas_call | solution.py:277
  139.1 7.5 %mask.1.m_ref = bf16[2,1024,1024]{2,1,0:T(8,128)(2,1)} custom-call(s32[8,8]{1,0:T(8,128)} %bitcast.32, f32[1024,1024]{1,0:T(8,128)} %bitcast.4.panel_ref), custom_call_target="tpu_custom_call" | custom-call | flops 1 | bytes 1 | tf_op jit(solution)/shard_map/mask/pallas_call | solution.py:290
  146.6 10.8 %turn.1.t_ref = bf16[2,1024,1024]{2,1,0:T(8,128)(2,1)} custom-call(f32[1024,1024]{1,0:T(8,128)} %cov.1.cov_ref, bf16[2,1024,1024]{2,1,0:T(8,128)(2,1)} %mask.1.m_ref), custom_call_target="tpu_custom_call" | custom-call | flops 1 | bytes 1 | tf_op jit(solution)/shard_map/turn/pallas_call | solution.py:300
  157.5 9.7 %all-to-all-done.1 = f32[16,32,1024]{2,1,0:T(8,128)S(1)} async-done(((f32[16,32,1024]{2,1,0:T(8,128)}), f32[16,32,1024]{2,1,0:T(8,128)S(1)}, u32[]{:S(2)}, u32[]{:S(2)}) %all-to-all-start.1) | async-done | bytes 2097184 | tf_op jit(solution)/shard_map/all_to_all | solution.py:240
  167.1 7.1 %cross.1 = (f32[1024,1024]{1,0:T(8,128)}, bf16[2,1024,1024]{2,1,0:T(8,128)(2,1)}) custom-call(bf16[2,1024,1024]{2,1,0:T(8,128)(2,1)} %turn.1.t_ref, f32[512,1024]{1,0:T(8,128)S(1)} %bitcast.23), custom_call_target="tpu_custom_call" | custom-call | tf_op jit(solution)/shard_map/cross/pallas_call | solution.py:310
  174.3 4.9 %all-to-all-start.2 = ((f32[16,64,1024]{2,1,0:T(8,128)}), f32[16,64,1024]{2,1,0:T(8,128)}, u32[]{:S(2)}, u32[]{:S(2)}) async-start(f32[16,64,1024]{2,1,0:T(8,128)} %bitcast.24), calls=%async_computation.2 | async-start | bytes 8388608 | tf_op jit(solution)/shard_map/all_to_all | solution.py:240
  179.2 1.1 slice.50
  180.3 0.3 copy.19
  180.6 0.1 reshape.77
  180.7 0.1 select_reduce_fusion
  180.9 0.1 slice.45
  180.9 0.1 slice.47
  181.0 0.1 rev.7
  181.1 1.0 copy.16.weight_ref
  182.2 1.7 constant_dynamic-slice_fusion.1
  183.8 9.3 %variance.1 = f32[1,1024]{1,0:T(1,128)} custom-call(bf16[2,1024,1024]{2,1,0:T(8,128)(2,1)} %mask.1.m_ref, bf16[2,1024,1024]{2,1,0:T(8,128)(2,1)} %get-tuple-element.12.g_ref, f32[1024,1024]{1,0:T(8,128)} %get-tuple-element.11.cross_ref, f32[1024,1]{1,0:T(8,128)} %copy.16.weight_ref), custom_call_target="tpu_custom_call" | custom-call | tf_op jit(solution)/shard_map/variance/pallas_call | solution.py:351
  193.1 78.5 %all-to-all-done.2.from_ref = f32[16,64,1024]{2,1,0:T(8,128)} async-done(((f32[16,64,1024]{2,1,0:T(8,128)}), f32[16,64,1024]{2,1,0:T(8,128)}, u32[]{:S(2)}, u32[]{:S(2)}) %all-to-all-start.2) | async-done | bytes 4194336 | tf_op jit(solution)/shard_map/all_to_all | solution.py:240
  271.6 3.6 %place.1 = f32[16,64,1024]{2,1,0:T(8,128)} custom-call(f32[16,64,1024]{2,1,0:T(8,128)} %all-to-all-done.2.from_ref), custom_call_target="tpu_custom_call" | custom-call | tf_op jit(solution)/shard_map/place/pallas_call | solution.py:331
  (29 shorter events, 0.2 us)
Async XLA Ops:
  0.6 14.3 %collective-permute-start = (f32[64,1024]{1,0:T(8,128)}, f32[64,1024]{1,0:T(8,128)S(1)}, u32[]{:S(2)}, u32[]{:S(2)}) collective-permute-start(f32[64,1024]{1,0:T(8,128)} %param.7), channel_id=1, source_target_pairs={{0,8},{1,9},{2,10},{3,11},{4,12},{5,13},{6,14},{7,15},{8,0},{9,1},... | collective-permute-start | bytes 786440 | tf_op jit(solution)/shard_map/ppermute | solution.py:224
  4.4 17.7 %copy-start.3 = (f32[64,1024]{1,0:T(8,128)S(1)}, f32[64,1024]{1,0:T(8,128)}, u32[]{:S(2)}) copy-start(f32[64,1024]{1,0:T(8,128)} %param.7) | copy-start | bytes 786436
  4.4 10.5 %collective-permute-start.1 = (f32[1,1088]{1,0:T(1,128)S(1)}, f32[1,1088]{1,0:T(1,128)S(1)}, u32[]{:S(2)}, u32[]{:S(2)}) collective-permute-start(f32[1,1088]{1,0:T(1,128)S(1)} %broadcast_in_dim.44), channel_id=1, source_target_pairs={{0,8},{1,9},{2,10},{3,11},{4,12},{5,13},{6,14},{7,15},{8,0},{9,1},... | collective-permute-start | bytes 13064 | tf_op jit(solution)/shard_map/ppermute | solution.py:224
  15.0 99.9 %all-to-all-start = ((f32[16,64,1024]{2,1,0:T(8,128)}), f32[16,64,1024]{2,1,0:T(8,128)}, u32[]{:S(2)}, u32[]{:S(2)}) async-start(f32[16,64,1024]{2,1,0:T(8,128)} %param.10), calls=%async_computation | async-start | bytes 8388608 | tf_op jit(solution)/shard_map/all_to_all | solution.py:240
  22.1 4.8 %copy-start.2 = (f32[16,32,2,1024]{3,2,1,0:T(2,128)S(1)}, f32[16,32,2,1024]{3,2,1,0:T(2,128)}, u32[]{:S(2)}) copy-start(f32[16,32,2,1024]{3,2,1,0:T(2,128)} %param.11) | copy-start | bytes 12582916
  26.5 6.2 %copy-start.4 = (f32[288,1024]{1,0:T(8,128)}, f32[288,1024]{1,0:T(8,128)S(1)}, u32[]{:S(2)}) copy-start(f32[288,1024]{1,0:T(8,128)S(1)} %get-tuple-element.33) | copy-start | bytes 3538948
  26.6 32.0 %collective-permute-start.2 = (f32[144,1024]{1,0:T(8,128)S(1)}, f32[144,1024]{1,0:T(8,128)}, u32[]{:S(2)}, u32[]{:S(2)}) collective-permute-start(f32[144,1024]{1,0:T(8,128)S(1)} %pad_maximum_fusion), channel_id=1, source_target_pairs={{0,2},{1,3},{2,0},{3,1},{4,6},{5,7},{6,4},{7,5},{8,10},{9,11},{10,... | collective-permute-start | bytes 1769480 | tf_op jit(solution)/shard_map/ppermute | solution.py:224
  34.8 1.4 copy-start
  38.2 29.5 %copy-start.1 = (f32[16,32,1,1024]{3,1,0,2:T(8,128)S(1)}, f32[16,32,1,1024]{3,1,0,2:T(8,128)}, u32[]{:S(2)}) copy-start(f32[16,32,1,1024]{3,1,0,2:T(8,128)} %copy-done) | copy-start | bytes 6291460
  61.1 58.7 %collective-permute-start.3 = (f32[288,1024]{1,0:T(8,128)}, f32[288,1024]{1,0:T(8,128)S(1)}, u32[]{:S(2)}, u32[]{:S(2)}) collective-permute-start(f32[288,1024]{1,0:T(8,128)} %get-tuple-element.25), channel_id=1, source_target_pairs={{0,4},{1,5},{2,6},{3,7},{4,0},{5,1},{6,2},{7,3},{8,12},{9,13},{10,... | collective-permute-start | bytes 3538952 | tf_op jit(solution)/shard_map/ppermute | solution.py:224
  114.9 52.3 %all-to-all-start.1 = ((f32[16,32,1024]{2,1,0:T(8,128)}), f32[16,32,1024]{2,1,0:T(8,128)S(1)}, u32[]{:S(2)}, u32[]{:S(2)}) async-start(f32[16,32,1024]{2,1,0:T(8,128)} %fusion.2), calls=%async_computation.1 | async-start | bytes 4194304 | tf_op jit(solution)/shard_map/all_to_all | solution.py:240
  121.4 4.7 %collective-permute-start.4 = (f32[576,1024]{1,0:T(8,128)}, f32[576,1024]{1,0:T(8,128)S(1)}, u32[]{:S(2)}, u32[]{:S(2)}) collective-permute-start(f32[576,1024]{1,0:T(8,128)} %get-tuple-element.21), channel_id=1, source_target_pairs={{0,1},{1,0},{2,3},{3,2},{4,5},{5,4},{6,7},{7,6},{8,9},{9,8},{10,11... | collective-permute-start | bytes 7077896 | tf_op jit(solution)/shard_map/ppermute | solution.py:224
  174.2 4.9 %copy-start.5 = (s32[16]{0:T(128)S(1)}, s32[16]{0:T(128)}, u32[]{:S(2)}) copy-start(s32[16]{0:T(128)} %constant.66.clone) | copy-start | bytes 196
  174.3 97.4 %all-to-all-start.2 = ((f32[16,64,1024]{2,1,0:T(8,128)}), f32[16,64,1024]{2,1,0:T(8,128)}, u32[]{:S(2)}, u32[]{:S(2)}) async-start(f32[16,64,1024]{2,1,0:T(8,128)} %bitcast.24), calls=%async_computation.2 | async-start | bytes 8388608 | tf_op jit(solution)/shard_map/all_to_all | solution.py:240
